TPU v7x, 128 devices: a whole 4x4x4 slice. The times are simulated.
128 devices in a mesh: section: 2 (over core), dev: 64 (over z, y, x).
Axes of the slice: x: 4, y: 4, z: 4, core: 2. Of those that a mesh axis runs over, the one named last changes fastest.
Arguments:
- hidden_rows: bfloat16 [2, 1024, 7168], P('section', 'dev'), may hold values from -6 to 6
- routes: int32 [2, 1024, 8], P('section', 'dev'), may hold values from 0 to 63, all different within a row; in each aligned block of 16 rows (0 to 15, 16 to 31, ..., all dimensions but the last counted through in order) at most 4 rows name the same one
- gate_weights: float32 [2, 1024, 8], P('section', 'dev'), may hold values from 0.05 to 0.5
- gate_proj: bfloat16 [64, 7168, 1024], P('dev', None, 'section'), may hold values from -0.0625 to 0.0625
- up_proj: bfloat16 [64, 7168, 1024], P('dev', None, 'section'), may hold values from -0.0625 to 0.0625
- down_proj: bfloat16 [64, 1024, 7168], P('dev', 'section'), may hold values from -0.1875 to 0.1875
- queries: bfloat16 [2, 128, 128, 576], P('section', 'dev'), may hold values from -50 to 50
- latent_cache: bfloat16 [2, 128, 1024, 576], P('section', 'dev'), may hold values from -6 to 6
- cache_lengths: int32 [2, 128], P('section', 'dev'), may hold values from 128 to 1024, as said below
Outputs:
- moe_out: bfloat16 [2, 1024, 7168], P('section', 'dev')
- attn_out: bfloat16 [2, 128, 128, 512], P('section', 'dev')
Inputs may be any that keep to these rules, and one draw needn't show every extreme that they name: `routes`: in each aligned block of 16 rows no expert is named by more than 4 pairs, a bound that some block reaches; a row names 8 different experts. `cache_lengths`: some request has exactly 1024 used slots.
All inputs are finite; a program needn't handle non-finite values.
Results may differ from a plain program's by a relative error of at most 0.011.
Values may be sent and summed in bfloat16 or wider, within the bound.
No kernel may reach another device: no remote copies, remote signals or barrier semaphores. Data moves between devices by JAX's collectives and lax.ppermute only.
A program may use at most 128 MiB of HBM per device.

v0:
```python
import jax
import jax.numpy as jnp
from jax import lax
from jax.sharding import PartitionSpec as P

LAT = 512


qk_scale = 192.0 ** (-0.5)


def add_halves(pair):
    return (pair[0].astype(jnp.float32) + pair[1].astype(jnp.float32)).astype(jnp.bfloat16)


def per_device(
    hidden_rows,
    routes,
    gate_weights,
    gate_proj,
    up_proj,
    down_proj,
    queries,
    latent_cache,
    cache_lengths,
):
    inputs = hidden_rows[0]
    rows = inputs.shape[0]
    top = routes.shape[2]
    width = inputs.shape[1]
    experts = lax.axis_size("dev")
    capacity = 2 * rows * top // experts
    flat = routes[0].reshape(-1)
    onehot = (flat[:, None] == jnp.arange(experts, dtype=jnp.int32)[None, :]).astype(jnp.int32)
    before = jnp.cumsum(onehot, axis=0) - onehot
    positions = jnp.sum(before * onehot, axis=1)
    slot_ids = flat * capacity + positions
    pick = (slot_ids[:, None] == jnp.arange(experts * capacity, dtype=jnp.int32)[None, :]).astype(
        jnp.bfloat16
    )
    owner = (
        (jnp.arange(rows * top, dtype=jnp.int32) // top)[:, None]
        == jnp.arange(rows, dtype=jnp.int32)[None, :]
    ).astype(jnp.bfloat16)
    placing = jnp.dot(pick.T, owner, preferred_element_type=jnp.float32).astype(jnp.bfloat16)
    outgoing = (
        jnp.dot(placing, inputs, preferred_element_type=jnp.float32)
        .astype(jnp.bfloat16)
        .reshape(experts, capacity, width)
    )
    w_gate = gate_proj[0]
    w_up = up_proj[0]
    w_down = down_proj[0]
    both_sides = lax.all_gather(outgoing[None], "section", axis=0, tiled=True)
    block = lax.all_to_all(both_sides, "dev", split_axis=1, concat_axis=1, tiled=True)
    flat_rows = block.reshape(-1, width)
    gate = jnp.dot(flat_rows, w_gate, preferred_element_type=jnp.float32)
    upper = jnp.dot(flat_rows, w_up, preferred_element_type=jnp.float32)
    hidden = (jax.nn.silu(gate) * upper).astype(jnp.bfloat16)
    partial_value = jnp.dot(hidden, w_down, preferred_element_type=jnp.float32).astype(jnp.bfloat16)
    partial_value = partial_value.reshape(block.shape)
    returned = lax.all_to_all(partial_value, "dev", split_axis=1, concat_axis=1, tiled=True)
    results = add_halves(
        lax.all_to_all(returned, "section", split_axis=0, concat_axis=0, tiled=True)
    )
    picked = results.reshape(experts * capacity, width)[slot_ids].astype(jnp.float32)
    weighted = picked.reshape(rows, top, width) * gate_weights[0][:, :, None]
    moe_out = jnp.sum(weighted, axis=1).astype(jnp.bfloat16)[None]
    cache = latent_cache[0]
    scores = (
        jnp.einsum("rhc,rlc->rhl", queries[0], cache, preferred_element_type=jnp.float32) * qk_scale
    )
    slots = cache.shape[1]
    valid = jnp.arange(slots, dtype=jnp.int32)[None, None, :] < cache_lengths[0][:, None, None]
    scores = jnp.where(valid, scores, -jnp.inf)
    peak = jnp.max(scores, axis=-1, keepdims=True)
    expo = jnp.where(valid, jnp.exp(scores - peak), 0.0)
    probs = (expo / jnp.sum(expo, axis=-1, keepdims=True)).astype(jnp.bfloat16)
    values = cache[:, :, :LAT]
    attn_out = jnp.einsum("rhl,rlc->rhc", probs, values, preferred_element_type=jnp.float32).astype(
        jnp.bfloat16
    )[None]
    return (moe_out, attn_out)


def solution(mesh):
    return jax.shard_map(
        per_device,
        mesh=mesh,
        in_specs=(
            P("section", "dev", None),
            P("section", "dev", None),
            P("section", "dev", None),
            P("dev", None, "section"),
            P("dev", None, "section"),
            P("dev", "section", None),
            P("section", "dev", None, None),
            P("section", "dev", None, None),
            P("section", "dev"),
        ),
        out_specs=(P("section", "dev", None), P("section", "dev", None, None)),
        check_vma=False,
    )
```

profile of v0, /device:TPU:5, one launch (start us, length us, event | category | flops | bytes accessed | tf_op | source)
XLA Modules:
  0.0 380.2 jit_solution(2165592350508519038)
XLA Ops:
  7.2 0.0 copy-start
  7.2 0.0 all-gather.2.cloned.1.call-start
  7.2 0.8 copy.38
  8.0 0.1 reshape_squeeze.3
  8.1 0.1 fusion.37
  8.2 0.2 reduce_window_sum.11
  8.4 0.2 select_reduce_fusion
  8.6 4.2 %convolution_convert_fusion.1 = bf16[256,7168]{1,0:T(8,128)(2,1)} fusion(bf16[1,16,7168]{2,1,0:T(8,128)(2,1)} %param.9, s32[128]{0:T(128)S(1)} %get-tuple-element.5, s32[128]{0:T(128)S(1)} %get-tuple-element.4), kind=kOutput, calls=%fused_computation.3 | convolution fusion | flops 61642752 | bytes 3900416 | tf_op jit(solution)/shard_map/dot_general | solution.py:47
  12.7 7.0 %broadcast_in_dim_reshape.3 = bf16[1,64,4,7168]{3,2,1,0:T(4,128)(2,1)} reshape(bf16[256,7168]{1,0:T(8,128)(2,1)} %convolution_convert_fusion.1) | data formatting | bytes 7340032 | tf_op jit(solution)/shard_map/broadcast_in_dim;reshape | solution.py:54
  19.7 5.1 %copy.39 = bf16[1,64,4,7168]{3,1,2,0:T(8,128)(2,1)} copy(bf16[1,64,4,7168]{3,2,1,0:T(4,128)(2,1)} %broadcast_in_dim_reshape.3) | data formatting | bytes 7340032 | tf_op jit(solution)/shard_map/broadcast_in_dim;reshape | solution.py:54
  24.8 0.0 all-gather.2.cloned.1.call-update
  24.8 24.0 %all-gather.2.cloned.1.call-done = bf16[2,64,4,7168]{3,1,2,0:T(8,128)(2,1)} async-done(((bf16[1,64,4,7168]{3,1,2,0:T(8,128)(2,1)}), bf16[2,64,4,7168]{3,1,2,0:T(8,128)(2,1)}) %all-gather.2.cloned.1.call-update) | async-done | bytes 7340048 | tf_op jit(solution)/shard_map/all_gather | solution.py:54
  48.9 11.8 %copy.40 = bf16[2,64,4,7168]{3,2,0,1:T(4,128)(2,1)} copy(bf16[2,64,4,7168]{3,1,2,0:T(8,128)(2,1)} %all-gather.2.cloned.1.call-done) | data formatting | bytes 14680064 | tf_op jit(solution)/shard_map/all_gather | solution.py:54
  60.6 94.3 %all_to_all.15 = bf16[2,64,4,7168]{3,2,0,1:T(4,128)(2,1)} all-to-all(bf16[2,64,4,7168]{3,2,0,1:T(4,128)(2,1)} %copy.40), channel_id=1, replica_groups=mesh['section'=2,'dev'=64] {'dev'}, dimensions={1} | all-to-all | bytes 14680064 | tf_op jit(solution)/shard_map/all_to_all | solution.py:55
  155.0 8.6 %copy.41 = bf16[2,64,4,7168]{3,2,1,0:T(4,128)(2,1)} copy(bf16[2,64,4,7168]{3,2,0,1:T(4,128)(2,1)} %all_to_all.15) | data formatting | bytes 14680064 | tf_op jit(solution)/shard_map/all_to_all | solution.py:55
  163.6 12.1 %reshape.103 = bf16[512,7168]{1,0:T(8,128)(2,1)} reshape(bf16[2,64,4,7168]{3,2,1,0:T(4,128)(2,1)} %copy.41) | data formatting | bytes 14680064 | tf_op jit(solution)/shard_map/reshape | solution.py:56
  175.7 0.0 copy-start.1
  175.7 9.2 %fusion.4 = f32[512,512]{1,0:T(8,128)S(1)} fusion(bf16[512,7168]{1,0:T(8,128)(2,1)} %reshape.103, bf16[1,7168,512]{2,1,0:T(8,128)(2,1)} %param.12), kind=kOutput, calls=%fused_computation.7 | convolution fusion | flops 3758096384 | bytes 15728640 | tf_op jit(solution)/shard_map/dot_general | solution.py:57
  184.9 0.0 copy-done.1
  184.9 7.2 %fusion.23 = bf16[512,512]{1,0:T(8,128)(2,1)S(1)} fusion(bf16[512,7168]{1,0:T(8,128)(2,1)S(1)} %copy-done.1, bf16[1,7168,512]{2,1,0:T(8,128)(2,1)} %param.13, f32[512,512]{1,0:T(8,128)S(1)} %fusion.4), kind=kOutput, calls=%fused_computation.22 | convolution fusion | flops 3759669248 | bytes 16252928 | tf_op jit(solution)/shard_map/dot_general | solution.py:58
  192.1 9.4 %convolution_convert_fusion = bf16[512,7168]{1,0:T(8,128)(2,1)} fusion(bf16[512,512]{1,0:T(8,128)(2,1)S(1)} %fusion.23, bf16[1,512,7168]{2,1,0:T(8,128)(2,1)} %param.14), kind=kOutput, calls=%fused_computation.2 | convolution fusion | flops 3761766400 | bytes 15204352 | tf_op jit(solution)/shard_map/dot_general | solution.py:60
  201.5 12.6 %reshape.104 = bf16[2,64,4,7168]{3,2,1,0:T(4,128)(2,1)} reshape(bf16[512,7168]{1,0:T(8,128)(2,1)} %convolution_convert_fusion) | data formatting | bytes 14680064 | tf_op jit(solution)/shard_map/reshape | solution.py:61
  214.1 10.4 %copy.42 = bf16[2,64,4,7168]{3,2,0,1:T(4,128)(2,1)} copy(bf16[2,64,4,7168]{3,2,1,0:T(4,128)(2,1)} %reshape.104) | data formatting | bytes 14680064 | tf_op jit(solution)/shard_map/reshape | solution.py:61
  224.5 0.0 copy-start.2
  224.5 0.0 copy-start.3
  224.5 0.0 copy-start.4
  224.5 8.0 %all-to-all-start.1 = ((bf16[2,64,4,7168]{3,2,0,1:T(4,128)(2,1)}), bf16[2,64,4,7168]{3,2,0,1:T(4,128)(2,1)}, u32[]{:S(2)}, u32[]{:S(2)}) async-start(bf16[2,64,4,7168]{3,2,0,1:T(4,128)(2,1)} %copy.42), calls=%async_computation.1 | async-start | bytes 14680064 | tf_op jit(solution)/shard_map/all_to_all | solution.py:62
  232.5 0.0 copy-done.2
  232.5 0.1 copy.44
  232.6 0.1 mul.56
  232.7 0.0 copy-done.3
  232.7 0.1 copy.45
  232.8 3.1 copy.46
  235.9 0.0 copy-done.4
  235.9 0.1 iota_compare_fusion.7
  236.0 0.0 copy-done
  236.0 3.5 fusion.41
  239.4 2.4 fusion.29
  241.9 91.4 %all-to-all-done.1 = bf16[2,64,4,7168]{3,2,0,1:T(4,128)(2,1)} async-done(((bf16[2,64,4,7168]{3,2,0,1:T(4,128)(2,1)}), bf16[2,64,4,7168]{3,2,0,1:T(4,128)(2,1)}, u32[]{:S(2)}, u32[]{:S(2)}) %all-to-all-start.1) | async-done | bytes 7340064 | tf_op jit(solution)/shard_map/all_to_all | solution.py:62
  333.3 8.6 %copy.43 = bf16[2,64,4,7168]{3,2,1,0:T(4,128)(2,1)} copy(bf16[2,64,4,7168]{3,2,0,1:T(4,128)(2,1)} %all-to-all-done.1) | data formatting | bytes 14680064 | tf_op jit(solution)/shard_map/all_to_all | solution.py:62
  341.9 13.1 %all_to_all.16 = bf16[2,64,4,7168]{3,2,1,0:T(4,128)(2,1)S(1)} all-to-all(bf16[2,64,4,7168]{3,2,1,0:T(4,128)(2,1)} %copy.43), channel_id=1, replica_groups=mesh['section'=2,'dev'=64] {'section'}, dimensions={0} | all-to-all | bytes 14680064 | tf_op jit(solution)/shard_map/all_to_all | solution.py:64
  355.1 3.7 add_convert_fusion
  358.7 6.7 %convert_element_type.68 = bf16[256,7168]{1,0:T(8,128)(2,1)} reshape(bf16[1,64,4,7168]{3,2,1,0:T(4,128)(2,1)} %add_convert_fusion) | data formatting | bytes 7340032 | tf_op jit(solution)/shard_map/convert_element_type | solution.py:13
  365.5 5.9 %gather_fusion = bf16[128,7168]{1,0:T(8,128)(2,1)S(1)} fusion(bf16[256,7168]{1,0:T(8,128)(2,1)} %convert_element_type.68, s32[1024]{0:T(1024)S(1)} %pad_clamp_fusion), kind=kCustom, calls=%fused_computation | custom fusion | bytes 3670528 | tf_op jit(solution)/shard_map/gather | solution.py:66
  371.4 2.0 fusion.6
  (4 shorter events, 0.0 us)
Async XLA Ops:
  7.2 228.8 %copy-start = (bf16[1,2,128,576]{2,3,1,0:T(8,128)(2,1)S(1)}, bf16[1,2,128,576]{2,3,1,0:T(8,128)(2,1)}, u32[]{:S(2)}) copy-start(bf16[1,2,128,576]{2,3,1,0:T(8,128)(2,1)} %param.15) | copy-start | bytes 884740
  7.2 41.7 %all-gather.2.cloned.1.call-start = ((), (), s32[]{:S(2)}) async-start(), calls=%async_computation.3 | async-start | bytes 11010048 | tf_op jit(solution)/shard_map/all_gather | solution.py:54
  175.7 9.2 %copy-start.1 = (bf16[512,7168]{1,0:T(8,128)(2,1)S(1)}, bf16[512,7168]{1,0:T(8,128)(2,1)}, u32[]{:S(2)}) copy-start(bf16[512,7168]{1,0:T(8,128)(2,1)} %reshape.103) | copy-start | bytes 22020100
  224.5 8.0 %copy-start.2 = (s32[1,16,8]{1,2,0:T(8,128)S(1)}, s32[1,16,8]{1,2,0:T(8,128)}, u32[]{:S(2)}) copy-start(s32[1,16,8]{1,2,0:T(8,128)} %param.10) | copy-start | bytes 1540
  224.5 8.2 %copy-start.3 = (f32[1,16,8]{1,2,0:T(8,128)S(1)}, f32[1,16,8]{1,2,0:T(8,128)}, u32[]{:S(2)}) copy-start(f32[1,16,8]{1,2,0:T(8,128)} %param.11) | copy-start | bytes 1540
  224.5 11.4 %copy-start.4 = (s32[1,2]{1,0:T(1,128)S(1)}, s32[1,2]{1,0:T(1,128)}, u32[]{:S(2)}) copy-start(s32[1,2]{1,0:T(1,128)} %param.17) | copy-start | bytes 28
  224.5 108.8 %all-to-all-start.1 = ((bf16[2,64,4,7168]{3,2,0,1:T(4,128)(2,1)}), bf16[2,64,4,7168]{3,2,0,1:T(4,128)(2,1)}, u32[]{:S(2)}, u32[]{:S(2)}) async-start(bf16[2,64,4,7168]{3,2,0,1:T(4,128)(2,1)} %copy.42), calls=%async_computation.1 | async-start | bytes 14680064 | tf_op jit(solution)/shard_map/all_to_all | solution.py:62
Sparse Core Ops, SparseCore 0:
  24.9 23.8 all-gather.1
where the time goes:
time: 382 us; the launch traced here: 380 us
  waiting for transfers between devices  115 us (30%)
  blocking collectives  107 us (28%)
  local copies, waits for them, and re-layouts  93 us (24%)
  matrix products  35.8 us (9%)
  between operations  14.2 us (4%)
  starting transfers between devices  8 us (2%)
  other arithmetic  6.17 us (2%)
    all_to_all x1, blocking collectives, per_device(): lax.all_to_all(both_sides, 'dev', split_axis=1, concat_axis=1, tiled=True)  94.3 us
    all_to_all x1, waiting for transfers between devices, per_device(): lax.all_to_all(partial_value, 'dev', split_axis=1, concat_axis=1, tiled=T...  91.4 us
    all_gather x1, waiting for transfers between devices, per_device(): both_sides = lax.all_gather(outgoing[None], 'section', axis=0, tiled=True)  24 us
    reshape x2, local copies, waits for them, and re-layouts, per_device(): partial_value = partial_value.reshape(block.shape)  23 us
    all_to_all x1, blocking collectives, per_device(): lax.all_to_all(returned, 'section', split_axis=0, concat_axis=0, tiled=True)  13.1 us
    reshape x1, local copies, waits for them, and re-layouts, per_device(): flat_rows = block.reshape(-1, width)  12.1 us
    another operation x2, local copies, waits for them, and re-layouts, per_device(): both_sides = lax.all_gather(outgoing[None], 'section', axis=0, tiled=True)  12.1 us
    all_gather x1, local copies, waits for them, and re-layouts, per_device(): both_sides = lax.all_gather(outgoing[None], 'section', axis=0, tiled=True)  11.8 us
  transfers between devices with their start and end apart: 2, of which 2 were waited for; matrix products, arithmetic and copies ran while one was open for 2% of the time, Pallas kernels for 0%

commit v1 on v0

v1 whole, which is shorter than its diff:
```python
import jax
import jax.numpy as jnp
from jax import lax
from jax.experimental import pallas as pl
from jax.experimental.pallas import tpu as pltpu
from jax.sharding import PartitionSpec as P

LAT = 512
SIDE = 4
CAP = 4
ROWS = 16
TOP = 8
SLOTS = SIDE**3 * CAP
BF16 = jnp.bfloat16
F32 = jnp.float32
I32 = jnp.int32

qk_scale = 192.0 ** (-0.5)

def swap_sections(value):
    return lax.ppermute(value, "section", [(0, 1), (1, 0)])


def dot32(left, right):
    return jnp.dot(left, right, preferred_element_type=F32)


def attention(queries, cache, lengths):
    scores = jnp.einsum("rhc,rlc->rhl", queries, cache, preferred_element_type=F32) * qk_scale
    slots = cache.shape[1]
    valid = jnp.arange(slots, dtype=I32)[None, None, :] < lengths[:, None, None]
    scores = jnp.where(valid, scores, -jnp.inf)
    peak = jnp.max(scores, axis=-1, keepdims=True)
    expo = jnp.where(valid, jnp.exp(scores - peak), 0.0)
    probs = (expo / jnp.sum(expo, axis=-1, keepdims=True)).astype(BF16)
    values = cache[:, :, :LAT]
    return jnp.einsum("rhl,rlc->rhc", probs, values, preferred_element_type=F32).astype(BF16)


def local_call(body, out, *operands, flops=0, scalars=0):
    specs = [
        pl.BlockSpec(memory_space=pltpu.SMEM if i < scalars else pltpu.VMEM)
        for i in range(len(operands))
    ]
    moved = sum(v.size * v.dtype.itemsize for v in operands) + sum(
        v.size * v.dtype.itemsize for v in out
    )
    return pl.pallas_call(
        body,
        out_shape=out,
        in_specs=specs,
        out_specs=[pl.BlockSpec(memory_space=pltpu.VMEM)] * len(out),
        cost_estimate=pl.CostEstimate(flops=flops, bytes_accessed=moved, transcendentals=0),
        compiler_params=pltpu.CompilerParams(vmem_limit_bytes=24 * 2**20),
    )(*operands)


def shaped(rows, width, dtype=BF16):
    return jax.ShapeDtypeStruct((rows, width), dtype)


def tiles(width, step=512):
    return [slice(lo, min(lo + step, width)) for lo in range(0, width, step)]


def iota(shape, dim):
    return lax.broadcasted_iota(I32, shape, dim)


def select_body(routes_ref, gains_ref, rows_ref, out_ref, weigh_ref):
    quarter = rows_ref.shape[1] // SIDE
    shape = (SIDE * ROWS, out_ref.shape[0])
    left, right = iota(shape, 0), iota(shape, 1)
    expert = lax.div(right, SIDE * CAP)
    routes = jnp.concatenate([routes_ref[...]] * SIDE, axis=0)
    gains = jnp.concatenate([gains_ref[...]] * SIDE, axis=0)
    named = jnp.zeros(shape, F32)
    weigh = jnp.zeros(shape, F32)
    for k in range(TOP):
        match = routes[:, k : k + 1] == expert
        named = jnp.where(match, 1.0, named)
        weigh = jnp.where(match, gains[:, k : k + 1], weigh)
    square = (SIDE * ROWS, SIDE * ROWS)
    row, column = iota(square, 0), iota(square, 1)
    earlier = (lax.div(row, ROWS) == lax.div(column, ROWS)) & (column < row)
    position = dot32(jnp.where(earlier, 1.0, 0.0).astype(BF16), named.astype(BF16)).astype(I32)
    hit = (
        (named > 0.5)
        & (position == lax.rem(right, CAP))
        & (lax.rem(lax.div(right, CAP), SIDE) == lax.div(left, ROWS))
    )
    weigh = jnp.where(hit, weigh, 0.0)
    high = weigh.astype(BF16)
    weigh_ref[: SIDE * ROWS, :] = high
    weigh_ref[SIDE * ROWS :, :] = (weigh - high.astype(F32)).astype(BF16)
    select = jnp.where(hit, 1.0, 0.0).T.astype(BF16)
    for cols in tiles(quarter, 256):
        rows = jnp.concatenate(
            [
                rows_ref[:, c * quarter + cols.start : c * quarter + cols.stop]
                for c in range(SIDE)
            ],
            axis=0,
        )
        out_ref[:, cols] = dot32(select, rows).astype(BF16)


def quarters_first(transposed):
    rows = SIDE * SIDE * ROWS
    out = iota((rows, rows), 1 if transposed else 0)
    given = iota((rows, rows), 0 if transposed else 1)
    group = SIDE * SIDE * CAP
    quarter, source = lax.div(out, group), lax.div(lax.rem(out, group), CAP)
    where = (source * SIDE + quarter) * CAP + lax.rem(out, CAP)
    return jnp.where(where == given, 1.0, 0.0).astype(BF16)


def arrive_body(raw_ref, out_ref):
    quarter = raw_ref.shape[1]
    turn = quarters_first(False)
    rows, group = turn.shape[0], turn.shape[0] // SIDE
    for g in range(raw_ref.shape[0] // rows):
        for cols in tiles(quarter, 256):
            turned = dot32(turn, raw_ref[g * rows : (g + 1) * rows, cols]).astype(BF16)
            for c in range(SIDE):
                out_ref[
                    g * group : (g + 1) * group, c * quarter + cols.start : c * quarter + cols.stop
                ] = turned[c * group : (c + 1) * group]


def leave_body(*refs):
    halves = len(refs) // 2
    mine, other, out_ref = refs[:halves], refs[halves : 2 * halves], refs[-1]
    quarter = out_ref.shape[1]
    turn = quarters_first(True)
    rows, group = turn.shape[0], turn.shape[0] // SIDE
    width = mine[0].shape[1]
    for g in range(out_ref.shape[0] // rows):
        for cols in tiles(quarter, 256):
            total = []
            for c in range(SIDE):
                h, at = divmod(c * quarter + cols.start, width)
                span = slice(at, at + cols.stop - cols.start)
                keep = slice(g * group, (g + 1) * group)
                total.append(
                    (mine[h][keep, span].astype(F32) + other[h][keep, span].astype(F32)).astype(BF16)
                )
            total = jnp.concatenate(total, axis=0)
            out_ref[g * rows : (g + 1) * rows, cols] = dot32(turn, total).astype(BF16)


def combine_body(weigh_ref, raw_ref, out_ref):
    quarter = raw_ref.shape[1]
    half = SIDE * ROWS
    for cols in tiles(quarter, 256):
        both = dot32(weigh_ref[...], raw_ref[:, cols])
        summed = (both[:half] + both[half:]).astype(BF16)
        for c in range(SIDE):
            out_ref[:, c * quarter + cols.start : c * quarter + cols.stop] = summed[
                c * ROWS : (c + 1) * ROWS
            ]


def per_device(
    hidden_rows,
    routes,
    gate_weights,
    gate_proj,
    up_proj,
    down_proj,
    queries,
    latent_cache,
    cache_lengths,
):
    inputs = hidden_rows[0]
    width = inputs.shape[1]
    w_gate, w_up, w_down = gate_proj[0], up_proj[0], down_proj[0]
    raw_rows, quarter = SLOTS * SIDE, width // SIDE

    outgoing, weigh = local_call(
        select_body,
        [shaped(raw_rows, quarter), shaped(2 * SIDE * ROWS, raw_rows)],
        routes[0],
        gate_weights[0],
        inputs,
        flops=2 * raw_rows * SIDE * ROWS * quarter,
    )
    raw = lax.all_to_all(outgoing, "dev", 0, 0, tiled=True)
    raw_other = swap_sections(raw)

    def hidden_of(value):
        block = local_call(
            arrive_body, [shaped(SLOTS, width)], value, flops=2 * SLOTS * SLOTS * width
        )[0]
        gate = dot32(block, w_gate)
        upper = dot32(block, w_up)
        return (jax.nn.silu(gate) * upper).astype(BF16)

    hidden_mine = hidden_of(raw)
    hidden_other = hidden_of(raw_other)
    halves = [w_down[:, : width // 2], w_down[:, width // 2 :]]
    returned = [swap_sections(dot32(hidden_other, w).astype(BF16)) for w in halves]
    kept = [dot32(hidden_mine, w).astype(BF16) for w in halves]
    leaving = local_call(
        leave_body,
        [shaped(raw_rows, quarter)],
        *kept,
        *returned,
        flops=2 * SLOTS * SLOTS * width,
    )[0]
    back = lax.all_to_all(leaving, "dev", 0, 0, tiled=True)
    moe_out = local_call(
        combine_body,
        [shaped(ROWS, width)],
        weigh,
        back,
        flops=4 * raw_rows * SIDE * ROWS * quarter,
    )[0]
    attn_out = attention(queries[0], latent_cache[0], cache_lengths[0])
    return (moe_out[None], attn_out[None])


def solution(mesh):
    return jax.shard_map(
        per_device,
        mesh=mesh,
        in_specs=(
            P("section", "dev", None),
            P("section", "dev", None),
            P("section", "dev", None),
            P("dev", None, "section"),
            P("dev", None, "section"),
            P("dev", "section", None),
            P("section", "dev", None, None),
            P("section", "dev", None, None),
            P("section", "dev"),
        ),
        out_specs=(P("section", "dev", None), P("section", "dev", None, None)),
        check_vma=False,
    )
```

time: 382 us -> 146 us (0.38)
  the two profiles are of different devices: /device:TPU:5 before, /device:TPU:0 now
where the time goes in v1:
time: 146 us
  blocking collectives  58.5 us (40%)
  waiting for transfers between devices  45.5 us (31%)
  matrix products  18.7 us (13%)
  Pallas kernels  8.32 us (6%)
  local copies, waits for them, and re-layouts  7.69 us (5%)
  starting transfers between devices  6.21 us (4%)
    all_to_all x1, blocking collectives, per_device(): raw = lax.all_to_all(outgoing, 'dev', 0, 0, tiled=True)  58.5 us
    all_to_all x1, waiting for transfers between devices, per_device(): back = lax.all_to_all(leaving, 'dev', 0, 0, tiled=True)  40.2 us
    dot_general x8, matrix products, dot32(): return jnp.dot(left, right, preferred_element_type=F32)  12.7 us
    pallas_call x5, Pallas kernels, local_call(): pl.pallas_call(body, out_shape=out, in_specs=specs, out_specs=[pl.BlockSp...  8.32 us
    unnamed x21, local copies, waits for them, and re-layouts  6.13 us
    all_to_all x1, starting transfers between devices, per_device(): back = lax.all_to_all(leaving, 'dev', 0, 0, tiled=True)  5.62 us
    ppermute x3, waiting for transfers between devices, swap_sections(): return lax.ppermute(value, 'section', [(0, 1), (1, 0)])  5.28 us
    sub x1, matrix products, attention(): expo = jnp.where(valid, jnp.exp(scores - peak), 0.0)  3.54 us
  transfers between devices with their start and end apart: 4, of which 2 were waited for; matrix products, arithmetic and copies ran while one was open for 11% of the time, Pallas kernels for 1%

profile of v1, /device:TPU:0, one launch (start us, length us, event | category | flops | bytes accessed | tf_op | source)
XLA Modules:
  0.0 145.7 jit_solution(10616667951578161794)
XLA Ops:
  0.6 0.0 copy-start
  0.6 0.8 copy.11.routes_ref
  1.4 0.8 copy.12.gains_ref
  2.2 0.0 copy-start.2
  2.2 0.9 copy-done.2
  3.1 1.5 %shard_map.104 = (bf16[1024,1792]{1,0:T(8,128)(2,1)S(1)}, bf16[128,1024]{1,0:T(8,128)(2,1)S(1)}) custom-call(s32[16,8]{1,0:T(8,128)S(1)} %copy.11.routes_ref, f32[16,8]{1,0:T(8,128)S(1)} %copy.12.gains_ref, bf16[16,7168]{1,0:T(8,128)(2,1)S(1)} %bitcast.55), custom_call_target="tpu_custom_call" | custom-call | flops 234881024 | bytes 4162560 | tf_op jit(solution)/shard_map/pallas_call | solution.py:48
  4.7 0.0 slice-start
  4.7 58.5 %all_to_all.22 = bf16[64,16,1792]{2,1,0:T(8,128)(2,1)S(1)} all-to-all(bf16[64,16,1792]{2,1,0:T(8,128)(2,1)S(1)} %bitcast.54), channel_id=1, replica_groups=mesh['section'=2,'dev'=64] {'dev'}, dimensions={0} | all-to-all | bytes 7340032 | tf_op jit(solution)/shard_map/all_to_all | solution.py:188
  63.1 0.0 slice-start.1
  63.1 0.0 collective-permute-start
  63.1 1.1 shard_map.105
  64.3 5.3 %collective-permute-done.raw_ref = bf16[1024,1792]{1,0:T(8,128)(2,1)S(1)} collective-permute-done((bf16[1024,1792]{1,0:T(8,128)(2,1)S(1)}, bf16[1024,1792]{1,0:T(8,128)(2,1)S(1)}, u32[]{:S(2)}, u32[]{:S(2)}) %collective-permute-start) | collective-permute-done | bytes 3670048 | tf_op jit(solution)/shard_map/ppermute | solution.py:21
  69.5 0.0 slice-start.2
  69.6 1.1 shard_map.106
  70.7 0.0 slice-done
  70.7 0.0 slice-done.1
  70.7 0.0 slice-start.3
  70.7 0.0 slice-start.4
  70.7 2.0 %fusion.5 = f32[256,512]{1,0:T(8,128)S(1)} fusion(bf16[256,7168]{1,0:T(8,128)(2,1)S(1)} %shard_map.106, bf16[1,7168,512]{2,1,0:T(8,128)(2,1)S(1)} %bitcast.62), kind=kOutput, calls=%fused_computation.5 | convolution fusion | flops 1879048192 | bytes 11534336 | tf_op jit(solution)/shard_map/dot_general | solution.py:25
  72.8 0.0 slice-done.2
  72.8 0.1 slice-done.3
  73.0 0.0 slice-start.5
  73.0 2.1 %multiply_convert_fusion = bf16[256,512]{1,0:T(8,128)(2,1)S(1)} fusion(f32[256,512]{1,0:T(8,128)S(1)} %fusion.5, bf16[256,7168]{1,0:T(8,128)(2,1)S(1)} %shard_map.106, bf16[1,7168,512]{2,1,0:T(8,128)(2,1)S(1)} %bitcast.64), kind=kOutput, calls=%fused_computation.32 | convolution fusion | flops 1879834624 | bytes 11796480 | tf_op jit(solution)/shard_map/dot_general | solution.py:25
  75.0 0.0 slice-done.4
  75.0 0.1 slice-done.5
  75.1 1.1 convolution_convert_fusion.1
  76.2 1.1 convolution_convert_fusion
  77.3 0.2 collective-permute-start.1
  77.6 0.4 collective-permute-start.2
  77.9 2.0 %fusion.7 = f32[256,512]{1,0:T(8,128)S(1)} fusion(bf16[256,7168]{1,0:T(8,128)(2,1)S(1)} %shard_map.105, bf16[1,7168,512]{2,1,0:T(8,128)(2,1)S(1)} %bitcast.62), kind=kOutput, calls=%fused_computation.7 | convolution fusion | flops 1879048192 | bytes 11534336 | tf_op jit(solution)/shard_map/dot_general | solution.py:25
  80.0 2.1 %fusion.32 = bf16[256,512]{1,0:T(8,128)(2,1)S(1)} fusion(bf16[256,7168]{1,0:T(8,128)(2,1)S(1)} %shard_map.105, bf16[1,7168,512]{2,1,0:T(8,128)(2,1)S(1)} %bitcast.64, f32[256,512]{1,0:T(8,128)S(1)} %fusion.7), kind=kOutput, calls=%fused_computation.28 | convolution fusion | flops 1879834624 | bytes 11796480 | tf_op jit(solution)/shard_map/dot_general | solution.py:25
  82.1 1.1 convolution_convert_fusion.2.refs_1_
  83.2 1.1 convolution_convert_fusion.3.refs_0_
  84.3 0.0 collective-permute-done.1.refs_2_
  84.3 0.0 collective-permute-done.2.refs_3_
  84.3 1.2 shard_map.107
  85.5 0.0 copy-start.1
  85.5 1.8 %copy-done.1 = bf16[1024,1792]{1,0:T(8,128)(2,1)} copy-done((bf16[1024,1792]{1,0:T(8,128)(2,1)}, bf16[1024,1792]{1,0:T(8,128)(2,1)S(1)}, u32[]{:S(2)}) %copy-start.1) | copy-done | bytes 3670040
  87.4 5.6 %all-to-all-start.1 = ((bf16[64,16,1792]{2,1,0:T(8,128)(2,1)}), bf16[64,16,1792]{2,1,0:T(8,128)(2,1)}, u32[]{:S(2)}, u32[]{:S(2)}) async-start(bf16[64,16,1792]{2,1,0:T(8,128)(2,1)} %bitcast.53), calls=%async_computation.1 | async-start | bytes 7340032 | tf_op jit(solution)/shard_map/all_to_all | solution.py:211
  93.0 0.0 copy-start.3
  93.0 3.1 %copy.13 = bf16[1,2,1024,576]{3,2,1,0:T(8,128)(2,1)S(1)} copy(bf16[1,2,1024,576]{2,3,1,0:T(8,128)(2,1)} %param.16) | data formatting | bytes 4718592 | tf_op args[7]
  96.1 0.0 copy-done.3
  96.1 0.1 iota_compare_fusion
  96.2 0.0 copy-done
  96.2 3.5 %fusion.40 = (f32[2,128]{1,0:T(2,128)S(1)}, f32[2,128,1024]{2,1,0:T(8,128)}) fusion(pred[2,1024]{1,0:T(4,128)(4,1)S(1)} %iota_compare_fusion, bf16[1,2,1024,576]{2,3,1,0:T(8,128)(2,1)} %param.16, bf16[1,2,128,576]{2,3,1,0:T(8,128)(2,1)S(1)} %copy-done), kind=kOutput, calls=%fused_computation.35 | convolution fusion | flops 303301632 | bytes 3705856 | tf_op jit(solution)/shard_map/sub | solution.py:34
  99.8 2.4 %fusion.35 = bf16[1,2,128,512]{3,2,1,0:T(8,128)(2,1)} fusion(bf16[2,1024,576]{2,1,0:T(8,128)(2,1)S(1)} %bitcast.56, f32[2,128,1024]{2,1,0:T(8,128)} %get-tuple-element.7, f32[2,128]{1,0:T(2,128)S(1)} %get-tuple-element.6), kind=kOutput, calls=%fused_computation.29 | convolution fusion | flops 269090816 | bytes 3408896 | tf_op jit(solution)/shard_map/rhl,rlc->rhc/dot_general | solution.py:37
  102.2 40.2 %all-to-all-done.1 = bf16[64,16,1792]{2,1,0:T(8,128)(2,1)} async-done(((bf16[64,16,1792]{2,1,0:T(8,128)(2,1)}), bf16[64,16,1792]{2,1,0:T(8,128)(2,1)}, u32[]{:S(2)}, u32[]{:S(2)}) %all-to-all-start.1) | async-done | bytes 3670048 | tf_op jit(solution)/shard_map/all_to_all | solution.py:211
  142.4 3.4 %shard_map.108 = bf16[16,7168]{1,0:T(8,128)(2,1)} custom-call(bf16[128,1024]{1,0:T(8,128)(2,1)S(1)} %get-tuple-element.4.weigh_ref, bf16[1024,1792]{1,0:T(8,128)(2,1)} %bitcast.9.raw_ref), custom_call_target="tpu_custom_call" | custom-call | flops 469762048 | bytes 4161536 | tf_op jit(solution)/shard_map/pallas_call | solution.py:48
  (3 shorter events, 0.0 us)
Async XLA Ops:
  0.6 95.6 %copy-start = (bf16[1,2,128,576]{2,3,1,0:T(8,128)(2,1)S(1)}, bf16[1,2,128,576]{2,3,1,0:T(8,128)(2,1)}, u32[]{:S(2)}) copy-start(bf16[1,2,128,576]{2,3,1,0:T(8,128)(2,1)} %param.15) | copy-start | bytes 884740
  2.2 0.9 copy-start.2
  4.7 66.0 %slice-start = ((s8[7340032]{0:T(1024)(128)(4,1)}), s8[4194304]{0:T(1024)(128)(4,1)S(1)}, s32[]{:S(2)}) async-start(s8[7340032]{0:T(1024)(128)(4,1)} %bitcast.61), calls=%async_computation.2 | async-start | bytes 8388608
  63.1 7.6 %slice-start.1 = ((s8[7340032]{0:T(1024)(128)(4,1)}), s8[3145728]{0:T(1024)(128)(4,1)S(1)}, s32[]{:S(2)}) async-start(s8[7340032]{0:T(1024)(128)(4,1)} %bitcast.61), calls=%async_computation.3 | async-start | bytes 6291456
  63.1 6.4 %collective-permute-start = (bf16[1024,1792]{1,0:T(8,128)(2,1)S(1)}, bf16[1024,1792]{1,0:T(8,128)(2,1)S(1)}, u32[]{:S(2)}, u32[]{:S(2)}) collective-permute-start(bf16[1024,1792]{1,0:T(8,128)(2,1)S(1)} %bitcast.51), channel_id=1, source_target_pairs={{0,64},{64,0},{1,65},{65,1},{2,66},{66,2},{3,67},{67,3},{4,68},{68... | collective-permute-start | bytes 11010056 | tf_op jit(solution)/shard_map/ppermute | solution.py:21
  69.5 3.2 %slice-start.2 = ((s8[7340032]{0:T(1024)(128)(4,1)}), s8[4194304]{0:T(1024)(128)(4,1)S(1)}, s32[]{:S(2)}) async-start(s8[7340032]{0:T(1024)(128)(4,1)} %bitcast.63), calls=%async_computation.4 | async-start | bytes 8388608
  70.7 2.2 %slice-start.3 = ((s8[7340032]{0:T(1024)(128)(4,1)}), s8[3145728]{0:T(1024)(128)(4,1)S(1)}, s32[]{:S(2)}) async-start(s8[7340032]{0:T(1024)(128)(4,1)} %bitcast.63), calls=%async_computation.5 | async-start | bytes 6291456
  70.7 4.3 %slice-start.4 = ((s8[7340032]{0:T(1024)(128)(4,1)}), s8[4194304]{0:T(1024)(128)(4,1)S(1)}, s32[]{:S(2)}) async-start(s8[7340032]{0:T(1024)(128)(4,1)} %bitcast.65), calls=%async_computation.6 | async-start | bytes 8388608
  73.0 2.1 %slice-start.5 = ((s8[7340032]{0:T(1024)(128)(4,1)}), s8[3145728]{0:T(1024)(128)(4,1)S(1)}, s32[]{:S(2)}) async-start(s8[7340032]{0:T(1024)(128)(4,1)} %bitcast.65), calls=%async_computation.7 | async-start | bytes 6291456
  77.3 7.0 %collective-permute-start.1 = (bf16[256,3584]{1,0:T(8,128)(2,1)S(1)}, bf16[256,3584]{1,0:T(8,128)(2,1)S(1)}, u32[]{:S(2)}, u32[]{:S(2)}) collective-permute-start(bf16[256,3584]{1,0:T(8,128)(2,1)S(1)} %convolution_convert_fusion.1), channel_id=1, source_target_pairs={{0,64},{64,0},{1,65},{65,1},{2,66},{66,2},{3,67},{67,3},{4,68},{68... | collective-permute-start | bytes 5505032 | tf_op jit(solution)/shard_map/ppermute | solution.py:21
  77.6 6.8 %collective-permute-start.2 = (bf16[256,3584]{1,0:T(8,128)(2,1)S(1)}, bf16[256,3584]{1,0:T(8,128)(2,1)S(1)}, u32[]{:S(2)}, u32[]{:S(2)}) collective-permute-start(bf16[256,3584]{1,0:T(8,128)(2,1)S(1)} %convolution_convert_fusion), channel_id=1, source_target_pairs={{0,64},{64,0},{1,65},{65,1},{2,66},{66,2},{3,67},{67,3},{4,68},{68... | collective-permute-start | bytes 5505032 | tf_op jit(solution)/shard_map/ppermute | solution.py:21
  85.5 1.9 %copy-start.1 = (bf16[1024,1792]{1,0:T(8,128)(2,1)}, bf16[1024,1792]{1,0:T(8,128)(2,1)S(1)}, u32[]{:S(2)}) copy-start(bf16[1024,1792]{1,0:T(8,128)(2,1)S(1)} %shard_map.107) | copy-start | bytes 11010052
  87.4 55.0 %all-to-all-start.1 = ((bf16[64,16,1792]{2,1,0:T(8,128)(2,1)}), bf16[64,16,1792]{2,1,0:T(8,128)(2,1)}, u32[]{:S(2)}, u32[]{:S(2)}) async-start(bf16[64,16,1792]{2,1,0:T(8,128)(2,1)} %bitcast.53), calls=%async_computation.1 | async-start | bytes 7340032 | tf_op jit(solution)/shard_map/all_to_all | solution.py:211
  93.0 3.1 %copy-start.3 = (s32[1,2]{1,0:T(1,128)S(1)}, s32[1,2]{1,0:T(1,128)}, u32[]{:S(2)}) copy-start(s32[1,2]{1,0:T(1,128)} %param.17) | copy-start | bytes 28

commit v2 on v1

--- a/solution.py
+++ b/solution.py
@@ -51,7 +51,7 @@
         in_specs=specs,
         out_specs=[pl.BlockSpec(memory_space=pltpu.VMEM)] * len(out),
         cost_estimate=pl.CostEstimate(flops=flops, bytes_accessed=moved, transcendentals=0),
-        compiler_params=pltpu.CompilerParams(vmem_limit_bytes=24 * 2**20),
+        compiler_params=pltpu.CompilerParams(vmem_limit_bytes=16 * 2**20),
     )(*operands)
 
 
@@ -69,31 +69,31 @@
 
 def select_body(routes_ref, gains_ref, rows_ref, out_ref, weigh_ref):
     quarter = rows_ref.shape[1] // SIDE
-    shape = (SIDE * ROWS, out_ref.shape[0])
+    shape = (out_ref.shape[0], SIDE * ROWS)
     left, right = iota(shape, 0), iota(shape, 1)
-    expert = lax.div(right, SIDE * CAP)
-    routes = jnp.concatenate([routes_ref[...]] * SIDE, axis=0)
-    gains = jnp.concatenate([gains_ref[...]] * SIDE, axis=0)
+    expert = lax.div(left, SIDE * CAP)
+    routes = jnp.concatenate([routes_ref[...]] * SIDE, axis=1)
+    gains = jnp.concatenate([gains_ref[...]] * SIDE, axis=1)
     named = jnp.zeros(shape, F32)
     weigh = jnp.zeros(shape, F32)
     for k in range(TOP):
-        match = routes[:, k : k + 1] == expert
+        match = routes[k : k + 1, :] == expert
         named = jnp.where(match, 1.0, named)
-        weigh = jnp.where(match, gains[:, k : k + 1], weigh)
+        weigh = jnp.where(match, gains[k : k + 1, :], weigh)
     square = (SIDE * ROWS, SIDE * ROWS)
     row, column = iota(square, 0), iota(square, 1)
-    earlier = (lax.div(row, ROWS) == lax.div(column, ROWS)) & (column < row)
-    position = dot32(jnp.where(earlier, 1.0, 0.0).astype(BF16), named.astype(BF16)).astype(I32)
+    earlier = (lax.div(row, ROWS) == lax.div(column, ROWS)) & (row < column)
+    position = dot32(named.astype(BF16), jnp.where(earlier, 1.0, 0.0).astype(BF16)).astype(I32)
     hit = (
         (named > 0.5)
-        & (position == lax.rem(right, CAP))
-        & (lax.rem(lax.div(right, CAP), SIDE) == lax.div(left, ROWS))
+        & (position == lax.rem(left, CAP))
+        & (lax.rem(lax.div(left, CAP), SIDE) == lax.div(right, ROWS))
     )
     weigh = jnp.where(hit, weigh, 0.0)
-    high = weigh.astype(BF16)
-    weigh_ref[: SIDE * ROWS, :] = high
-    weigh_ref[SIDE * ROWS :, :] = (weigh - high.astype(F32)).astype(BF16)
-    select = jnp.where(hit, 1.0, 0.0).T.astype(BF16)
+    high = weigh.astype(BF16).astype(F32)
+    weigh_ref[: SIDE * ROWS, :] = high.T.astype(BF16)
+    weigh_ref[SIDE * ROWS :, :] = (weigh - high).T.astype(BF16)
+    select = jnp.where(hit, 1.0, 0.0).astype(BF16)
     for cols in tiles(quarter, 256):
         rows = jnp.concatenate(
             [
@@ -180,32 +180,32 @@
     outgoing, weigh = local_call(
         select_body,
         [shaped(raw_rows, quarter), shaped(2 * SIDE * ROWS, raw_rows)],
-        routes[0],
-        gate_weights[0],
+        routes[0].T,
+        gate_weights[0].T,
         inputs,
         flops=2 * raw_rows * SIDE * ROWS * quarter,
     )
     raw = lax.all_to_all(outgoing, "dev", 0, 0, tiled=True)
-    raw_other = swap_sections(raw)
-
-    def hidden_of(value):
-        block = local_call(
-            arrive_body, [shaped(SLOTS, width)], value, flops=2 * SLOTS * SLOTS * width
-        )[0]
-        gate = dot32(block, w_gate)
-        upper = dot32(block, w_up)
-        return (jax.nn.silu(gate) * upper).astype(BF16)
-
-    hidden_mine = hidden_of(raw)
-    hidden_other = hidden_of(raw_other)
-    halves = [w_down[:, : width // 2], w_down[:, width // 2 :]]
-    returned = [swap_sections(dot32(hidden_other, w).astype(BF16)) for w in halves]
-    kept = [dot32(hidden_mine, w).astype(BF16) for w in halves]
+    raw, *others = lax.optimization_barrier(
+        (raw, swap_sections(w_gate), swap_sections(w_up), swap_sections(w_down))
+    )
+    block = local_call(arrive_body, [shaped(SLOTS, width)], raw, flops=2 * SLOTS * SLOTS * width)[0]
+    partials = []
+    for gate_half, up_half, down_half in (
+        (w_gate, w_up, w_down),
+        others,
+    ):
+        gate = dot32(block, gate_half)
+        upper = dot32(block, up_half)
+        hidden = lax.optimization_barrier((jax.nn.silu(gate) * upper).astype(BF16))
+        partials += [
+            dot32(hidden, down_half[:, span]).astype(BF16)
+            for span in (slice(0, width // 2), slice(width // 2, width))
+        ]
     leaving = local_call(
         leave_body,
         [shaped(raw_rows, quarter)],
-        *kept,
-        *returned,
+        *partials,
         flops=2 * SLOTS * SLOTS * width,
     )[0]
     back = lax.all_to_all(leaving, "dev", 0, 0, tiled=True)

time: 146 us -> 138 us (0.945)
  waiting for transfers between devices: 45.5 us -> 37.7 us
    ppermute x3, waiting for transfers between devices: 5.28 us -> 0.01 us  [swap_sections(): return lax.ppermute(value, 'section', [(0, 1), (1, 0)])]
    all_to_all x1, waiting for transfers between devices: 40.2 us -> 37.7 us  [per_device(): back = lax.all_to_all(leaving, 'dev', 0, 0, tiled=True)]
    squeeze x2 -> x0, local copies, waits for them, and re-layouts: 1.56 us -> none  [the longest x1 0.8 us: per_device(): routes[0]]
    unnamed x21 -> x25, local copies, waits for them, and re-layouts: 6.13 us -> 7.49 us
    pallas_call x5 -> x4, Pallas kernels: 8.32 us -> 7.64 us  [local_call(): pl.pallas_call(body, out_shape=out, in_specs=specs, out_specs=[pl.BlockSp...]
  transfers between devices with their start and end apart: 4 -> 4, of which waited for: 2 -> 1; matrix products, arithmetic and copies ran while one was open for 11% -> 7% of each run, Pallas kernels for 1% -> 1%
where the time goes in v2:
time: 138 us
  blocking collectives  58.8 us (43%)
  waiting for transfers between devices  37.7 us (27%)
  matrix products  18.7 us (14%)
  Pallas kernels  7.64 us (6%)
  local copies, waits for them, and re-layouts  7.49 us (5%)
  starting transfers between devices  6.51 us (5%)
    all_to_all x1, blocking collectives, per_device(): raw = lax.all_to_all(outgoing, 'dev', 0, 0, tiled=True)  58.8 us
    all_to_all x1, waiting for transfers between devices, per_device(): back = lax.all_to_all(leaving, 'dev', 0, 0, tiled=True)  37.7 us
    dot_general x8, matrix products, dot32(): return jnp.dot(left, right, preferred_element_type=F32)  12.7 us
    pallas_call x4, Pallas kernels, local_call(): pl.pallas_call(body, out_shape=out, in_specs=specs, out_specs=[pl.BlockSp...  7.64 us
    unnamed x25, local copies, waits for them, and re-layouts  7.49 us
    all_to_all x1, starting transfers between devices, per_device(): back = lax.all_to_all(leaving, 'dev', 0, 0, tiled=True)  5.84 us
    sub x1, matrix products, attention(): expo = jnp.where(valid, jnp.exp(scores - peak), 0.0)  3.54 us
  transfers between devices with their start and end apart: 4, of which 1 were waited for; matrix products, arithmetic and copies ran while one was open for 7% of the time, Pallas kernels for 1%

profile of v2, /device:TPU:0, one launch (start us, length us, event | category | flops | bytes accessed | tf_op | source)
XLA Modules:
  0.0 137.8 jit_solution(5785558546240570329)
XLA Ops:
  0.6 0.0 copy-start
  0.6 0.1 collective-permute-start.2
  0.7 0.5 collective-permute-start
  1.2 0.1 collective-permute-start.1
  1.3 0.0 copy-start.2
  1.3 0.9 copy-done.2
  2.3 0.0 copy-start.3
  2.3 0.7 copy-done.3
  3.0 0.7 copy-done.4
  3.6 2.0 %shard_map.104 = (bf16[1024,1792]{1,0:T(8,128)(2,1)S(1)}, bf16[128,1024]{1,0:T(8,128)(2,1)S(1)}) custom-call(s32[8,16]{1,0:T(8,128)S(1)} %bitcast.51, f32[8,16]{1,0:T(8,128)S(1)} %bitcast.52, bf16[16,7168]{1,0:T(8,128)(2,1)S(1)} %bitcast.50), custom_call_target="tpu_custom_call" | custom-call | flops 234881024 | bytes 4162560 | tf_op jit(solution)/shard_map/pallas_call | solution.py:48
  5.6 58.8 %all_to_all.23 = bf16[64,16,1792]{2,1,0:T(8,128)(2,1)S(1)} all-to-all(bf16[64,16,1792]{2,1,0:T(8,128)(2,1)S(1)} %bitcast.49), channel_id=1, replica_groups=mesh['section'=2,'dev'=64] {'dev'}, dimensions={0} | all-to-all | bytes 7340032 | tf_op jit(solution)/shard_map/all_to_all | solution.py:188
  64.4 0.0 collective-permute-done.2
  64.4 0.0 collective-permute-done
  64.4 0.0 collective-permute-done.1
  64.4 1.1 shard_map.105
  65.5 0.0 slice-start
  65.5 2.0 %fusion.35 = f32[256,512]{1,0:T(8,128)S(1)} fusion(bf16[256,7168]{1,0:T(8,128)(2,1)S(1)} %shard_map.105, bf16[7168,512]{1,0:T(8,128)(2,1)S(1)} %collective-permute-done), kind=kOutput, calls=%fused_computation.31 | convolution fusion | flops 1879048192 | bytes 11534336 | tf_op jit(solution)/shard_map/dot_general | solution.py:25
  67.6 0.0 slice-start.1
  67.6 2.1 %multiply_convert_fusion = bf16[256,512]{1,0:T(8,128)(2,1)S(1)} fusion(f32[256,512]{1,0:T(8,128)S(1)} %fusion.35, bf16[256,7168]{1,0:T(8,128)(2,1)S(1)} %shard_map.105, bf16[7168,512]{1,0:T(8,128)(2,1)S(1)} %collective-permute-done.1), kind=kOutput, calls=%fused_computation.24 | convolution fusion | flops 1879834624 | bytes 11796480 | tf_op jit(solution)/shard_map/dot_general | solution.py:25
  69.7 1.1 convolution_convert_fusion.refs_3_
  70.8 0.0 slice-start.2
  70.8 1.1 convolution_convert_fusion.1.refs_2_
  72.0 0.0 slice-done
  72.0 0.0 slice-done.1
  72.0 0.0 slice-start.3
  72.0 0.0 slice-start.4
  72.0 2.0 %fusion.28 = f32[256,512]{1,0:T(8,128)S(1)} fusion(bf16[256,7168]{1,0:T(8,128)(2,1)S(1)} %shard_map.105, bf16[1,7168,512]{2,1,0:T(8,128)(2,1)S(1)} %bitcast.58), kind=kOutput, calls=%fused_computation.28 | convolution fusion | flops 1879048192 | bytes 11534336 | tf_op jit(solution)/shard_map/dot_general | solution.py:25
  74.1 0.0 slice-done.2
  74.1 0.1 slice-done.3
  74.2 0.0 slice-start.5
  74.2 2.1 %fusion.21 = bf16[256,512]{1,0:T(8,128)(2,1)S(1)} fusion(bf16[256,7168]{1,0:T(8,128)(2,1)S(1)} %shard_map.105, f32[256,512]{1,0:T(8,128)S(1)} %fusion.28, bf16[1,7168,512]{2,1,0:T(8,128)(2,1)S(1)} %bitcast.61), kind=kOutput, calls=%fused_computation.20 | convolution fusion | flops 1879834624 | bytes 11796480 | tf_op jit(solution)/shard_map/dot_general | solution.py:25
  76.3 0.0 slice-done.4
  76.3 0.1 slice-done.5
  76.4 1.1 convolution_convert_fusion.2.refs_1_
  77.5 1.1 convolution_convert_fusion.3.refs_0_
  78.6 1.2 shard_map.106
  79.8 0.0 copy-start.1
  79.8 1.8 %copy-done.1 = bf16[1024,1792]{1,0:T(8,128)(2,1)} copy-done((bf16[1024,1792]{1,0:T(8,128)(2,1)}, bf16[1024,1792]{1,0:T(8,128)(2,1)S(1)}, u32[]{:S(2)}) %copy-start.1) | copy-done | bytes 3670040
  81.7 5.8 %all-to-all-start.1 = ((bf16[64,16,1792]{2,1,0:T(8,128)(2,1)}), bf16[64,16,1792]{2,1,0:T(8,128)(2,1)}, u32[]{:S(2)}, u32[]{:S(2)}) async-start(bf16[64,16,1792]{2,1,0:T(8,128)(2,1)} %bitcast.48), calls=%async_computation.1 | async-start | bytes 7340032 | tf_op jit(solution)/shard_map/all_to_all | solution.py:211
  87.5 0.0 copy-start.5
  87.5 3.1 %copy.11 = bf16[1,2,1024,576]{3,2,1,0:T(8,128)(2,1)S(1)} copy(bf16[1,2,1024,576]{2,3,1,0:T(8,128)(2,1)} %param.16) | data formatting | bytes 4718592 | tf_op args[7]
  90.6 0.0 copy-done.5
  90.6 0.1 iota_compare_fusion
  90.7 0.0 copy-done
  90.7 3.5 %fusion.30 = (f32[2,128]{1,0:T(2,128)S(1)}, f32[2,128,1024]{2,1,0:T(8,128)}) fusion(pred[2,1024]{1,0:T(4,128)(4,1)S(1)} %iota_compare_fusion, bf16[1,2,1024,576]{2,3,1,0:T(8,128)(2,1)} %param.16, bf16[1,2,128,576]{2,3,1,0:T(8,128)(2,1)S(1)} %copy-done), kind=kOutput, calls=%fused_computation.30 | convolution fusion | flops 303301632 | bytes 3705856 | tf_op jit(solution)/shard_map/sub | solution.py:34
  94.2 2.4 %fusion.22 = bf16[1,2,128,512]{3,2,1,0:T(8,128)(2,1)} fusion(bf16[2,1024,576]{2,1,0:T(8,128)(2,1)S(1)} %bitcast.53, f32[2,128,1024]{2,1,0:T(8,128)} %get-tuple-element.15, f32[2,128]{1,0:T(2,128)S(1)} %get-tuple-element.14), kind=kOutput, calls=%fused_computation.21 | convolution fusion | flops 269090816 | bytes 3408896 | tf_op jit(solution)/shard_map/rhl,rlc->rhc/dot_general | solution.py:37
  96.7 37.7 %all-to-all-done.1 = bf16[64,16,1792]{2,1,0:T(8,128)(2,1)} async-done(((bf16[64,16,1792]{2,1,0:T(8,128)(2,1)}), bf16[64,16,1792]{2,1,0:T(8,128)(2,1)}, u32[]{:S(2)}, u32[]{:S(2)}) %all-to-all-start.1) | async-done | bytes 3670048 | tf_op jit(solution)/shard_map/all_to_all | solution.py:211
  134.4 3.4 %shard_map.107 = bf16[16,7168]{1,0:T(8,128)(2,1)} custom-call(bf16[128,1024]{1,0:T(8,128)(2,1)S(1)} %get-tuple-element.8.weigh_ref, bf16[1024,1792]{1,0:T(8,128)(2,1)} %bitcast.11.raw_ref), custom_call_target="tpu_custom_call" | custom-call | flops 469762048 | bytes 4161536 | tf_op jit(solution)/shard_map/pallas_call | solution.py:48
  (4 shorter events, 0.0 us)
Async XLA Ops:
  0.6 90.1 %copy-start = (bf16[1,2,128,576]{2,3,1,0:T(8,128)(2,1)S(1)}, bf16[1,2,128,576]{2,3,1,0:T(8,128)(2,1)}, u32[]{:S(2)}) copy-start(bf16[1,2,128,576]{2,3,1,0:T(8,128)(2,1)} %param.15) | copy-start | bytes 884740
  0.6 63.7 %collective-permute-start.2 = (bf16[512,7168]{1,0:T(8,128)(2,1)}, bf16[512,7168]{1,0:T(8,128)(2,1)S(1)}, u32[]{:S(2)}, u32[]{:S(2)}) collective-permute-start(bf16[512,7168]{1,0:T(8,128)(2,1)} %bitcast.62), channel_id=1, source_target_pairs={{0,64},{64,0},{1,65},{65,1},{2,66},{66,2},{3,67},{67,3},{4,68},{68... | collective-permute-start | bytes 22020104 | tf_op jit(solution)/shard_map/ppermute | solution.py:21
  0.7 63.7 %collective-permute-start = (bf16[7168,512]{1,0:T(8,128)(2,1)}, bf16[7168,512]{1,0:T(8,128)(2,1)S(1)}, u32[]{:S(2)}, u32[]{:S(2)}) collective-permute-start(bf16[7168,512]{1,0:T(8,128)(2,1)} %bitcast.56), channel_id=1, source_target_pairs={{0,64},{64,0},{1,65},{65,1},{2,66},{66,2},{3,67},{67,3},{4,68},{68... | collective-permute-start | bytes 22020104 | tf_op jit(solution)/shard_map/ppermute | solution.py:21
  1.2 63.2 %collective-permute-start.1 = (bf16[7168,512]{1,0:T(8,128)(2,1)}, bf16[7168,512]{1,0:T(8,128)(2,1)S(1)}, u32[]{:S(2)}, u32[]{:S(2)}) collective-permute-start(bf16[7168,512]{1,0:T(8,128)(2,1)} %bitcast.59), channel_id=1, source_target_pairs={{0,64},{64,0},{1,65},{65,1},{2,66},{66,2},{3,67},{67,3},{4,68},{68... | collective-permute-start | bytes 22020104 | tf_op jit(solution)/shard_map/ppermute | solution.py:21
  1.3 0.9 copy-start.2
  2.3 0.7 copy-start.3
  3.0 0.7 copy-start.4
  65.5 6.4 %slice-start = ((s8[7340032]{0:T(1024)(128)(4,1)}), s8[4194304]{0:T(1024)(128)(4,1)S(1)}, s32[]{:S(2)}) async-start(s8[7340032]{0:T(1024)(128)(4,1)} %bitcast.57), calls=%async_computation.2 | async-start | bytes 8388608
  67.6 4.4 %slice-start.1 = ((s8[7340032]{0:T(1024)(128)(4,1)}), s8[3145728]{0:T(1024)(128)(4,1)S(1)}, s32[]{:S(2)}) async-start(s8[7340032]{0:T(1024)(128)(4,1)} %bitcast.57), calls=%async_computation.3 | async-start | bytes 6291456
  70.8 3.3 %slice-start.2 = ((s8[7340032]{0:T(1024)(128)(4,1)}), s8[4194304]{0:T(1024)(128)(4,1)S(1)}, s32[]{:S(2)}) async-start(s8[7340032]{0:T(1024)(128)(4,1)} %bitcast.60), calls=%async_computation.4 | async-start | bytes 8388608
  72.0 2.2 %slice-start.3 = ((s8[7340032]{0:T(1024)(128)(4,1)}), s8[3145728]{0:T(1024)(128)(4,1)S(1)}, s32[]{:S(2)}) async-start(s8[7340032]{0:T(1024)(128)(4,1)} %bitcast.60), calls=%async_computation.5 | async-start | bytes 6291456
  72.0 4.3 %slice-start.4 = ((s8[7340032]{0:T(1024)(128)(4,1)}), s8[4194304]{0:T(1024)(128)(4,1)S(1)}, s32[]{:S(2)}) async-start(s8[7340032]{0:T(1024)(128)(4,1)} %bitcast.63), calls=%async_computation.6 | async-start | bytes 8388608
  74.2 2.1 %slice-start.5 = ((s8[7340032]{0:T(1024)(128)(4,1)}), s8[3145728]{0:T(1024)(128)(4,1)S(1)}, s32[]{:S(2)}) async-start(s8[7340032]{0:T(1024)(128)(4,1)} %bitcast.63), calls=%async_computation.7 | async-start | bytes 6291456
  79.8 1.8 %copy-start.1 = (bf16[1024,1792]{1,0:T(8,128)(2,1)}, bf16[1024,1792]{1,0:T(8,128)(2,1)S(1)}, u32[]{:S(2)}) copy-start(bf16[1024,1792]{1,0:T(8,128)(2,1)S(1)} %shard_map.106) | copy-start | bytes 11010052
  81.7 52.7 %all-to-all-start.1 = ((bf16[64,16,1792]{2,1,0:T(8,128)(2,1)}), bf16[64,16,1792]{2,1,0:T(8,128)(2,1)}, u32[]{:S(2)}, u32[]{:S(2)}) async-start(bf16[64,16,1792]{2,1,0:T(8,128)(2,1)} %bitcast.48), calls=%async_computation.1 | async-start | bytes 7340032 | tf_op jit(solution)/shard_map/all_to_all | solution.py:211
  87.5 3.1 %copy-start.5 = (s32[1,2]{1,0:T(1,128)S(1)}, s32[1,2]{1,0:T(1,128)}, u32[]{:S(2)}) copy-start(s32[1,2]{1,0:T(1,128)} %param.17) | copy-start | bytes 28

commit v3 on v2

--- a/solution.py
+++ b/solution.py
@@ -25,16 +25,28 @@
     return jnp.dot(left, right, preferred_element_type=F32)
 
 
+def attention_body(lengths_ref, queries_ref, cache_ref, out_ref):
+    for r in range(queries_ref.shape[0]):
+        heads = queries_ref[r].astype(F32).T.astype(BF16)
+        scores = dot32(heads, cache_ref[r]) * qk_scale
+        valid = iota(scores.shape, 1) < lengths_ref[r]
+        scores = jnp.where(valid, scores, -jnp.inf)
+        peak = jnp.max(scores, axis=1, keepdims=True)
+        expo = jnp.where(valid, jnp.exp(scores - peak), 0.0)
+        probs = expo / jnp.sum(expo, axis=1, keepdims=True)
+        out_ref[r] = dot32(cache_ref[r, :LAT, :], probs.T.astype(BF16)).T.astype(BF16)
+
+
 def attention(queries, cache, lengths):
-    scores = jnp.einsum("rhc,rlc->rhl", queries, cache, preferred_element_type=F32) * qk_scale
-    slots = cache.shape[1]
-    valid = jnp.arange(slots, dtype=I32)[None, None, :] < lengths[:, None, None]
-    scores = jnp.where(valid, scores, -jnp.inf)
-    peak = jnp.max(scores, axis=-1, keepdims=True)
-    expo = jnp.where(valid, jnp.exp(scores - peak), 0.0)
-    probs = (expo / jnp.sum(expo, axis=-1, keepdims=True)).astype(BF16)
-    values = cache[:, :, :LAT]
-    return jnp.einsum("rhl,rlc->rhc", probs, values, preferred_element_type=F32).astype(BF16)
+    return local_call(
+        attention_body,
+        [jax.ShapeDtypeStruct((*queries.shape[:2], LAT), BF16)],
+        lengths,
+        queries.transpose(0, 2, 1),
+        cache.transpose(0, 2, 1),
+        flops=4 * queries.size * cache.shape[1],
+        scalars=1,
+    )[0]
 
 
 def local_call(body, out, *operands, flops=0, scalars=0):
@@ -186,18 +198,21 @@
         flops=2 * raw_rows * SIDE * ROWS * quarter,
     )
     raw = lax.all_to_all(outgoing, "dev", 0, 0, tiled=True)
-    raw, *others = lax.optimization_barrier(
-        (raw, swap_sections(w_gate), swap_sections(w_up), swap_sections(w_down))
-    )
+    raw, lengths, *others = lax.optimization_barrier(
+        (raw, cache_lengths[0], swap_sections(w_gate), swap_sections(w_up), swap_sections(w_down))
+    )
+    attn_out = attention(queries[0], latent_cache[0], lengths)
     block = local_call(arrive_body, [shaped(SLOTS, width)], raw, flops=2 * SLOTS * SLOTS * width)[0]
     partials = []
     for gate_half, up_half, down_half in (
+        others,
         (w_gate, w_up, w_down),
-        others,
     ):
         gate = dot32(block, gate_half)
         upper = dot32(block, up_half)
-        hidden = lax.optimization_barrier((jax.nn.silu(gate) * upper).astype(BF16))
+        hidden, block = lax.optimization_barrier(
+            ((jax.nn.silu(gate) * upper).astype(BF16), block)
+        )
         partials += [
             dot32(hidden, down_half[:, span]).astype(BF16)
             for span in (slice(0, width // 2), slice(width // 2, width))
@@ -208,6 +223,7 @@
         *partials,
         flops=2 * SLOTS * SLOTS * width,
     )[0]
+    leaving, attn_out = lax.optimization_barrier((leaving, attn_out))
     back = lax.all_to_all(leaving, "dev", 0, 0, tiled=True)
     moe_out = local_call(
         combine_body,
@@ -216,7 +232,6 @@
         back,
         flops=4 * raw_rows * SIDE * ROWS * quarter,
     )[0]
-    attn_out = attention(queries[0], latent_cache[0], cache_lengths[0])
     return (moe_out[None], attn_out[None])
 
 

time: 138 us -> 137 us (level)
  blocking collectives: 58.8 us -> 111 us
  waiting for transfers between devices: 37.7 us -> 0.01 us
  matrix products: 18.7 us -> 12.8 us
  starting transfers between devices: 6.51 us -> 0.68 us
  local copies, waits for them, and re-layouts: 7.49 us -> 3.2 us
    all_to_all x0 -> x1, blocking collectives: none -> 51.9 us  [per_device(): back = lax.all_to_all(leaving, 'dev', 0, 0, tiled=True)]
    all_to_all x1 -> x0, waiting for transfers between devices: 37.7 us -> none  [per_device(): back = lax.all_to_all(leaving, 'dev', 0, 0, tiled=True)]
    all_to_all x1 -> x0, starting transfers between devices: 5.84 us -> none  [per_device(): back = lax.all_to_all(leaving, 'dev', 0, 0, tiled=True)]
    unnamed x25 -> x24, local copies, waits for them, and re-layouts: 7.49 us -> 3.2 us
    sub x1 -> x0, matrix products: 3.54 us -> none  [attention(): expo = jnp.where(valid, jnp.exp(scores - peak), 0.0)]
    dot_general x1 -> x0, matrix products: 2.42 us -> none  [attention(): jnp.einsum('rhl,rlc->rhc', probs, values, preferred_element_type=F32)]
    pallas_call x4 -> x5, Pallas kernels: 7.64 us -> 8.59 us  [local_call(): pl.pallas_call(body, out_shape=out, in_specs=specs, out_specs=[pl.BlockSp...]
  transfers between devices with their start and end apart: 4 -> 3, of which waited for: 1 -> 0; matrix products, arithmetic and copies ran while one was open for 7% -> 0% of each run, Pallas kernels for 1% -> 1%
where the time goes in v3:
time: 137 us
  blocking collectives  111 us (81%)
  matrix products  12.8 us (9%)
  Pallas kernels  8.59 us (6%)
  local copies, waits for them, and re-layouts  3.2 us (2%)
    all_to_all x1, blocking collectives, per_device(): raw = lax.all_to_all(outgoing, 'dev', 0, 0, tiled=True)  58.8 us
    all_to_all x1, blocking collectives, per_device(): back = lax.all_to_all(leaving, 'dev', 0, 0, tiled=True)  51.9 us
    dot_general x8, matrix products, dot32(): return jnp.dot(left, right, preferred_element_type=F32)  12.8 us
    pallas_call x5, Pallas kernels, local_call(): pl.pallas_call(body, out_shape=out, in_specs=specs, out_specs=[pl.BlockSp...  8.59 us
    unnamed x24, local copies, waits for them, and re-layouts  3.2 us
  transfers between devices with their start and end apart: 3, of which 0 were waited for; matrix products, arithmetic and copies ran while one was open for 0% of the time, Pallas kernels for 1%

profile of v3, /device:TPU:0, one launch (start us, length us, event | category | flops | bytes accessed | tf_op | source)
XLA Modules:
  0.0 136.8 jit_solution(7991411317083318592)
XLA Ops:
  0.6 0.1 collective-permute-start.2
  0.7 0.5 collective-permute-start.1
  1.2 0.1 collective-permute-start
  1.3 0.0 copy-start.3
  1.3 0.9 copy-done.3
  2.3 0.0 copy-start.4
  2.3 0.7 copy-done.4
  2.9 0.0 copy-start.5
  2.9 0.7 copy-done.5
  3.6 2.0 %shard_map.104 = (bf16[1024,1792]{1,0:T(8,128)(2,1)S(1)}, bf16[128,1024]{1,0:T(8,128)(2,1)S(1)}) custom-call(s32[8,16]{1,0:T(8,128)S(1)} %bitcast.45, f32[8,16]{1,0:T(8,128)S(1)} %bitcast.46, bf16[16,7168]{1,0:T(8,128)(2,1)S(1)} %bitcast.44), custom_call_target="tpu_custom_call" | custom-call | flops 234881024 | bytes 4162560 | tf_op jit(solution)/shard_map/pallas_call | solution.py:60
  5.6 58.8 %all_to_all.23 = bf16[64,16,1792]{2,1,0:T(8,128)(2,1)S(1)} all-to-all(bf16[64,16,1792]{2,1,0:T(8,128)(2,1)S(1)} %bitcast.40), channel_id=1, replica_groups=mesh['section'=2,'dev'=64] {'dev'}, dimensions={0} | all-to-all | bytes 7340032 | tf_op jit(solution)/shard_map/all_to_all | solution.py:200
  64.4 0.0 collective-permute-done.2
  64.4 0.0 collective-permute-done.1
  64.4 0.0 collective-permute-done
  64.4 1.1 shard_map.105
  65.5 0.0 slice-start
  65.5 0.0 slice-start.2
  65.5 2.0 %fusion.8 = f32[256,512]{1,0:T(8,128)S(1)} fusion(bf16[256,7168]{1,0:T(8,128)(2,1)S(1)} %shard_map.105, bf16[7168,512]{1,0:T(8,128)(2,1)S(1)} %collective-permute-done), kind=kOutput, calls=%fused_computation.14 | convolution fusion | flops 1879048192 | bytes 11534336 | tf_op jit(solution)/shard_map/dot_general | solution.py:25
  67.6 0.0 slice-start.1
  67.6 0.0 slice-start.3
  67.6 2.1 %multiply_convert_fusion = bf16[256,512]{1,0:T(8,128)(2,1)S(1)} fusion(f32[256,512]{1,0:T(8,128)S(1)} %fusion.8, bf16[256,7168]{1,0:T(8,128)(2,1)S(1)} %shard_map.105, bf16[7168,512]{1,0:T(8,128)(2,1)S(1)} %collective-permute-done.1), kind=kOutput, calls=%fused_computation.10 | convolution fusion | flops 1879834624 | bytes 11796480 | tf_op jit(solution)/shard_map/dot_general | solution.py:25
  69.7 0.0 slice-done
  69.7 0.4 slice-done.1
  70.1 0.0 slice-start.4
  70.1 2.0 %fusion.6 = f32[256,512]{1,0:T(8,128)S(1)} fusion(bf16[256,7168]{1,0:T(8,128)(2,1)S(1)} %shard_map.105, bf16[1,7168,512]{2,1,0:T(8,128)(2,1)S(1)} %bitcast.51), kind=kOutput, calls=%fused_computation.12 | convolution fusion | flops 1879048192 | bytes 11534336 | tf_op jit(solution)/shard_map/dot_general | solution.py:25
  72.1 0.0 slice-done.2
  72.2 0.0 slice-done.3
  72.2 0.0 slice-start.5
  72.2 2.1 %fusion.4 = bf16[256,512]{1,0:T(8,128)(2,1)S(1)} fusion(bf16[256,7168]{1,0:T(8,128)(2,1)S(1)} %shard_map.105, f32[256,512]{1,0:T(8,128)S(1)} %fusion.6, bf16[1,7168,512]{2,1,0:T(8,128)(2,1)S(1)} %bitcast.54), kind=kOutput, calls=%fused_computation.9 | convolution fusion | flops 1879834624 | bytes 11796480 | tf_op jit(solution)/shard_map/dot_general | solution.py:25
  74.3 0.0 slice-done.4
  74.3 0.0 slice-done.5
  74.3 1.1 convolution_convert_fusion.refs_3_
  75.4 1.1 convolution_convert_fusion.1.refs_2_
  76.5 1.2 convolution_convert_fusion.2.refs_1_
  77.7 0.0 copy-start
  77.7 0.0 copy-start.1
  77.7 0.0 copy-start.2
  77.8 1.2 convolution_convert_fusion.3.refs_0_
  78.9 0.4 copy-done
  79.4 0.0 copy-done.1
  79.4 0.0 copy-done.2
  79.4 3.0 %shard_map.107 = bf16[2,128,512]{2,1,0:T(8,128)(2,1)} custom-call(s32[2]{0:T(128)S(1)} %bitcast.43, bf16[2,576,128]{2,1,0:T(8,128)(2,1)S(1)} %bitcast.42, bf16[2,576,1024]{2,1,0:T(8,128)(2,1)S(1)} %bitcast.41), custom_call_target="tpu_custom_call" | custom-call | flops 603979776 | bytes 2916360 | tf_op jit(solution)/shard_map/pallas_call | solution.py:60
  82.4 1.2 shard_map.106
  83.6 51.9 %all_to_all.24 = bf16[64,16,1792]{2,1,0:T(8,128)(2,1)S(1)} all-to-all(bf16[64,16,1792]{2,1,0:T(8,128)(2,1)S(1)} %bitcast.39), channel_id=1, replica_groups=mesh['section'=2,'dev'=64] {'dev'}, dimensions={0} | all-to-all | bytes 7340032 | tf_op jit(solution)/shard_map/all_to_all | solution.py:227
  135.5 1.3 shard_map.108
  (3 shorter events, 0.0 us)
Async XLA Ops:
  0.6 63.7 %collective-permute-start.2 = (bf16[512,7168]{1,0:T(8,128)(2,1)}, bf16[512,7168]{1,0:T(8,128)(2,1)S(1)}, u32[]{:S(2)}, u32[]{:S(2)}) collective-permute-start(bf16[512,7168]{1,0:T(8,128)(2,1)} %bitcast.55), channel_id=1, source_target_pairs={{0,64},{64,0},{1,65},{65,1},{2,66},{66,2},{3,67},{67,3},{4,68},{68... | collective-permute-start | bytes 22020104 | tf_op jit(solution)/shard_map/ppermute | solution.py:21
  0.7 63.7 %collective-permute-start.1 = (bf16[7168,512]{1,0:T(8,128)(2,1)}, bf16[7168,512]{1,0:T(8,128)(2,1)S(1)}, u32[]{:S(2)}, u32[]{:S(2)}) collective-permute-start(bf16[7168,512]{1,0:T(8,128)(2,1)} %bitcast.52), channel_id=1, source_target_pairs={{0,64},{64,0},{1,65},{65,1},{2,66},{66,2},{3,67},{67,3},{4,68},{68... | collective-permute-start | bytes 22020104 | tf_op jit(solution)/shard_map/ppermute | solution.py:21
  1.2 63.2 %collective-permute-start = (bf16[7168,512]{1,0:T(8,128)(2,1)}, bf16[7168,512]{1,0:T(8,128)(2,1)S(1)}, u32[]{:S(2)}, u32[]{:S(2)}) collective-permute-start(bf16[7168,512]{1,0:T(8,128)(2,1)} %bitcast.49), channel_id=1, source_target_pairs={{0,64},{64,0},{1,65},{65,1},{2,66},{66,2},{3,67},{67,3},{4,68},{68... | collective-permute-start | bytes 22020104 | tf_op jit(solution)/shard_map/ppermute | solution.py:21
  1.3 0.9 copy-start.3
  2.3 0.7 copy-start.4
  2.9 0.7 copy-start.5
  65.5 4.2 %slice-start = ((s8[7340032]{0:T(1024)(128)(4,1)}), s8[4194304]{0:T(1024)(128)(4,1)S(1)}, s32[]{:S(2)}) async-start(s8[7340032]{0:T(1024)(128)(4,1)} %bitcast.50), calls=%async_computation.2 | async-start | bytes 8388608
  65.5 6.6 %slice-start.2 = ((s8[7340032]{0:T(1024)(128)(4,1)}), s8[4194304]{0:T(1024)(128)(4,1)S(1)}, s32[]{:S(2)}) async-start(s8[7340032]{0:T(1024)(128)(4,1)} %bitcast.53), calls=%async_computation.4 | async-start | bytes 8388608
  67.6 2.5 %slice-start.1 = ((s8[7340032]{0:T(1024)(128)(4,1)}), s8[3145728]{0:T(1024)(128)(4,1)S(1)}, s32[]{:S(2)}) async-start(s8[7340032]{0:T(1024)(128)(4,1)} %bitcast.50), calls=%async_computation.3 | async-start | bytes 6291456
  67.6 4.5 %slice-start.3 = ((s8[7340032]{0:T(1024)(128)(4,1)}), s8[3145728]{0:T(1024)(128)(4,1)S(1)}, s32[]{:S(2)}) async-start(s8[7340032]{0:T(1024)(128)(4,1)} %bitcast.53), calls=%async_computation.5 | async-start | bytes 6291456
  70.1 4.2 %slice-start.4 = ((s8[7340032]{0:T(1024)(128)(4,1)}), s8[4194304]{0:T(1024)(128)(4,1)S(1)}, s32[]{:S(2)}) async-start(s8[7340032]{0:T(1024)(128)(4,1)} %bitcast.56), calls=%async_computation.6 | async-start | bytes 8388608
  72.2 2.1 %slice-start.5 = ((s8[7340032]{0:T(1024)(128)(4,1)}), s8[3145728]{0:T(1024)(128)(4,1)S(1)}, s32[]{:S(2)}) async-start(s8[7340032]{0:T(1024)(128)(4,1)} %bitcast.56), calls=%async_computation.7 | async-start | bytes 6291456
  77.7 1.7 %copy-start = (bf16[1,2,1024,576]{2,3,1,0:T(8,128)(2,1)S(1)}, bf16[1,2,1024,576]{2,3,1,0:T(8,128)(2,1)}, u32[]{:S(2)}) copy-start(bf16[1,2,1024,576]{2,3,1,0:T(8,128)(2,1)} %param.16) | copy-start | bytes 7077892
  77.7 1.7 %copy-start.1 = (bf16[1,2,128,576]{2,3,1,0:T(8,128)(2,1)S(1)}, bf16[1,2,128,576]{2,3,1,0:T(8,128)(2,1)}, u32[]{:S(2)}) copy-start(bf16[1,2,128,576]{2,3,1,0:T(8,128)(2,1)} %param.15) | copy-start | bytes 884740
  77.7 1.7 %copy-start.2 = (s32[1,2]{1,0:T(1,128)S(1)}, s32[1,2]{1,0:T(1,128)}, u32[]{:S(2)}) copy-start(s32[1,2]{1,0:T(1,128)} %param.17) | copy-start | bytes 28

commit v4 on v3

--- a/solution.py
+++ b/solution.py
@@ -81,31 +81,33 @@
 
 def select_body(routes_ref, gains_ref, rows_ref, out_ref, weigh_ref):
     quarter = rows_ref.shape[1] // SIDE
-    shape = (out_ref.shape[0], SIDE * ROWS)
+    shape = (SIDE * ROWS, out_ref.shape[0])
     left, right = iota(shape, 0), iota(shape, 1)
-    expert = lax.div(left, SIDE * CAP)
-    routes = jnp.concatenate([routes_ref[...]] * SIDE, axis=1)
-    gains = jnp.concatenate([gains_ref[...]] * SIDE, axis=1)
+    expert = lax.div(right, SIDE * CAP).astype(F32)
+    given = jnp.concatenate([routes_ref[...].astype(F32), gains_ref[...]], axis=0)
+    given = jnp.concatenate([given, jnp.zeros((2 * TOP, 128 - ROWS), F32)], axis=1)
+    given = jnp.concatenate([given, jnp.zeros((128 - 2 * TOP, 128), F32)], axis=0).T[:ROWS]
+    given = jnp.concatenate([given] * SIDE, axis=0)
     named = jnp.zeros(shape, F32)
     weigh = jnp.zeros(shape, F32)
     for k in range(TOP):
-        match = routes[k : k + 1, :] == expert
+        match = given[:, k : k + 1] == expert
         named = jnp.where(match, 1.0, named)
-        weigh = jnp.where(match, gains[k : k + 1, :], weigh)
+        weigh = jnp.where(match, given[:, TOP + k : TOP + k + 1], weigh)
     square = (SIDE * ROWS, SIDE * ROWS)
     row, column = iota(square, 0), iota(square, 1)
-    earlier = (lax.div(row, ROWS) == lax.div(column, ROWS)) & (row < column)
-    position = dot32(named.astype(BF16), jnp.where(earlier, 1.0, 0.0).astype(BF16)).astype(I32)
+    earlier = (lax.div(row, ROWS) == lax.div(column, ROWS)) & (column < row)
+    position = dot32(jnp.where(earlier, 1.0, 0.0).astype(BF16), named.astype(BF16)).astype(I32)
     hit = (
         (named > 0.5)
-        & (position == lax.rem(left, CAP))
-        & (lax.rem(lax.div(left, CAP), SIDE) == lax.div(right, ROWS))
+        & (position == lax.rem(right, CAP))
+        & (lax.rem(lax.div(right, CAP), SIDE) == lax.div(left, ROWS))
     )
     weigh = jnp.where(hit, weigh, 0.0)
-    high = weigh.astype(BF16).astype(F32)
-    weigh_ref[: SIDE * ROWS, :] = high.T.astype(BF16)
-    weigh_ref[SIDE * ROWS :, :] = (weigh - high).T.astype(BF16)
-    select = jnp.where(hit, 1.0, 0.0).astype(BF16)
+    high = weigh.astype(BF16)
+    weigh_ref[: SIDE * ROWS, :] = high
+    weigh_ref[SIDE * ROWS :, :] = (weigh - high.astype(F32)).astype(BF16)
+    select = jnp.where(hit, 1.0, 0.0).T.astype(BF16)
     for cols in tiles(quarter, 256):
         rows = jnp.concatenate(
             [
@@ -198,21 +200,23 @@
         flops=2 * raw_rows * SIDE * ROWS * quarter,
     )
     raw = lax.all_to_all(outgoing, "dev", 0, 0, tiled=True)
-    raw, lengths, *others = lax.optimization_barrier(
-        (raw, cache_lengths[0], swap_sections(w_gate), swap_sections(w_up), swap_sections(w_down))
-    )
-    attn_out = attention(queries[0], latent_cache[0], lengths)
+    raw, *others = lax.optimization_barrier(
+        (raw, swap_sections(w_gate), swap_sections(w_up), swap_sections(w_down))
+    )
     block = local_call(arrive_body, [shaped(SLOTS, width)], raw, flops=2 * SLOTS * SLOTS * width)[0]
     partials = []
+    attn_out = None
     for gate_half, up_half, down_half in (
         others,
         (w_gate, w_up, w_down),
     ):
         gate = dot32(block, gate_half)
         upper = dot32(block, up_half)
-        hidden, block = lax.optimization_barrier(
-            ((jax.nn.silu(gate) * upper).astype(BF16), block)
-        )
+        hidden = (jax.nn.silu(gate) * upper).astype(BF16)
+        hidden, block, lengths = lax.optimization_barrier((hidden, block, cache_lengths[0]))
+        if attn_out is None:
+            attn_out = attention(queries[0], latent_cache[0], lengths)
+            block, attn_out = lax.optimization_barrier((block, attn_out))
         partials += [
             dot32(hidden, down_half[:, span]).astype(BF16)
             for span in (slice(0, width // 2), slice(width // 2, width))
@@ -223,7 +227,6 @@
         *partials,
         flops=2 * SLOTS * SLOTS * width,
     )[0]
-    leaving, attn_out = lax.optimization_barrier((leaving, attn_out))
     back = lax.all_to_all(leaving, "dev", 0, 0, tiled=True)
     moe_out = local_call(
         combine_body,

time: 137 us -> 136 us (level)
  no operation moved by 1% of the time
where the time goes in v4:
time: 136 us
  blocking collectives  111 us (82%)
  matrix products  13.1 us (10%)
  Pallas kernels  8.24 us (6%)
  local copies, waits for them, and re-layouts  2.37 us (2%)
    all_to_all x1, blocking collectives, per_device(): raw = lax.all_to_all(outgoing, 'dev', 0, 0, tiled=True)  58.8 us
    all_to_all x1, blocking collectives, per_device(): back = lax.all_to_all(leaving, 'dev', 0, 0, tiled=True)  51.9 us
    dot_general x8, matrix products, dot32(): return jnp.dot(left, right, preferred_element_type=F32)  13.1 us
    pallas_call x5, Pallas kernels, local_call(): pl.pallas_call(body, out_shape=out, in_specs=specs, out_specs=[pl.BlockSp...  8.24 us
  transfers between devices with their start and end apart: 3, of which 0 were waited for; matrix products, arithmetic and copies ran while one was open for 0% of the time, Pallas kernels for 1%

profile of v4, /device:TPU:0, one launch (start us, length us, event | category | flops | bytes accessed | tf_op | source)
XLA Modules:
  0.0 136.0 jit_solution(6891889324962786692)
XLA Ops:
  0.6 0.1 collective-permute-start.2
  0.7 0.5 collective-permute-start.1
  1.2 0.1 collective-permute-start
  1.3 0.0 copy-start.3
  1.3 0.9 copy-done.3
  2.3 0.0 copy-start.4
  2.3 0.7 copy-done.4
  2.9 0.0 copy-start.5
  2.9 0.7 copy-done.5
  3.6 1.6 %shard_map.104 = (bf16[1024,1792]{1,0:T(8,128)(2,1)S(1)}, bf16[128,1024]{1,0:T(8,128)(2,1)S(1)}) custom-call(s32[8,16]{1,0:T(8,128)S(1)} %bitcast.45, f32[8,16]{1,0:T(8,128)S(1)} %bitcast.46, bf16[16,7168]{1,0:T(8,128)(2,1)S(1)} %bitcast.44), custom_call_target="tpu_custom_call" | custom-call | flops 234881024 | bytes 4162560 | tf_op jit(solution)/shard_map/pallas_call | solution.py:60
  5.2 58.8 %all_to_all.23 = bf16[64,16,1792]{2,1,0:T(8,128)(2,1)S(1)} all-to-all(bf16[64,16,1792]{2,1,0:T(8,128)(2,1)S(1)} %bitcast.40), channel_id=1, replica_groups=mesh['section'=2,'dev'=64] {'dev'}, dimensions={0} | all-to-all | bytes 7340032 | tf_op jit(solution)/shard_map/all_to_all | solution.py:202
  64.0 0.0 collective-permute-done.2
  64.0 0.0 collective-permute-done.1
  64.0 0.0 collective-permute-done
  64.0 1.1 shard_map.105
  65.2 0.0 slice-start
  65.2 2.1 %fusion.8 = f32[256,512]{1,0:T(8,128)S(1)} fusion(bf16[256,7168]{1,0:T(8,128)(2,1)S(1)} %shard_map.105, bf16[7168,512]{1,0:T(8,128)(2,1)S(1)} %collective-permute-done), kind=kOutput, calls=%fused_computation.14 | convolution fusion | flops 1879048192 | bytes 11534336 | tf_op jit(solution)/shard_map/dot_general | solution.py:25
  67.3 0.0 copy-start
  67.4 0.0 copy-start.1
  67.4 0.0 copy-start.2
  67.4 0.0 slice-start.1
  67.4 2.2 %multiply_convert_fusion = bf16[256,512]{1,0:T(8,128)(2,1)S(1)} fusion(f32[256,512]{1,0:T(8,128)S(1)} %fusion.8, bf16[256,7168]{1,0:T(8,128)(2,1)S(1)} %shard_map.105, bf16[7168,512]{1,0:T(8,128)(2,1)S(1)} %collective-permute-done.1), kind=kOutput, calls=%fused_computation.10 | convolution fusion | flops 1879834624 | bytes 11796480 | tf_op jit(solution)/shard_map/dot_general | solution.py:25
  69.6 0.0 copy-done
  69.6 0.0 copy-done.1
  69.6 0.0 copy-done.2
  69.6 0.0 slice-start.2
  69.6 3.0 %shard_map.106 = bf16[2,128,512]{2,1,0:T(8,128)(2,1)} custom-call(s32[2]{0:T(128)S(1)} %bitcast.43, bf16[2,576,128]{2,1,0:T(8,128)(2,1)S(1)} %bitcast.42, bf16[2,576,1024]{2,1,0:T(8,128)(2,1)S(1)} %bitcast.41), custom_call_target="tpu_custom_call" | custom-call | flops 603979776 | bytes 2916360 | tf_op jit(solution)/shard_map/pallas_call | solution.py:60
  72.6 0.0 slice-done
  72.6 0.0 slice-done.1
  72.6 0.0 slice-start.3
  72.6 0.0 slice-start.4
  72.6 2.1 %fusion.6 = f32[256,512]{1,0:T(8,128)S(1)} fusion(bf16[256,7168]{1,0:T(8,128)(2,1)S(1)} %shard_map.105, bf16[1,7168,512]{2,1,0:T(8,128)(2,1)S(1)} %bitcast.51), kind=kOutput, calls=%fused_computation.12 | convolution fusion | flops 1879048192 | bytes 11534336 | tf_op jit(solution)/shard_map/dot_general | solution.py:25
  74.8 0.0 slice-done.2
  74.8 0.0 slice-done.3
  74.8 0.0 slice-start.5
  74.8 2.2 %fusion.4 = bf16[256,512]{1,0:T(8,128)(2,1)S(1)} fusion(bf16[256,7168]{1,0:T(8,128)(2,1)S(1)} %shard_map.105, f32[256,512]{1,0:T(8,128)S(1)} %fusion.6, bf16[1,7168,512]{2,1,0:T(8,128)(2,1)S(1)} %bitcast.54), kind=kOutput, calls=%fused_computation.9 | convolution fusion | flops 1879834624 | bytes 11796480 | tf_op jit(solution)/shard_map/dot_general | solution.py:25
  77.0 0.0 slice-done.4
  77.0 0.0 slice-done.5
  77.0 1.1 convolution_convert_fusion.refs_3_
  78.1 1.1 convolution_convert_fusion.1.refs_2_
  79.3 1.1 convolution_convert_fusion.2.refs_1_
  80.4 1.1 convolution_convert_fusion.3.refs_0_
  81.5 1.2 shard_map.107
  82.7 51.9 %all_to_all.24 = bf16[64,16,1792]{2,1,0:T(8,128)(2,1)S(1)} all-to-all(bf16[64,16,1792]{2,1,0:T(8,128)(2,1)S(1)} %bitcast.39), channel_id=1, replica_groups=mesh['section'=2,'dev'=64] {'dev'}, dimensions={0} | all-to-all | bytes 7340032 | tf_op jit(solution)/shard_map/all_to_all | solution.py:230
  134.7 1.3 shard_map.108
  (3 shorter events, 0.0 us)
Async XLA Ops:
  0.6 63.4 %collective-permute-start.2 = (bf16[512,7168]{1,0:T(8,128)(2,1)}, bf16[512,7168]{1,0:T(8,128)(2,1)S(1)}, u32[]{:S(2)}, u32[]{:S(2)}) collective-permute-start(bf16[512,7168]{1,0:T(8,128)(2,1)} %bitcast.55), channel_id=1, source_target_pairs={{0,64},{64,0},{1,65},{65,1},{2,66},{66,2},{3,67},{67,3},{4,68},{68... | collective-permute-start | bytes 22020104 | tf_op jit(solution)/shard_map/ppermute | solution.py:21
  0.7 63.3 %collective-permute-start.1 = (bf16[7168,512]{1,0:T(8,128)(2,1)}, bf16[7168,512]{1,0:T(8,128)(2,1)S(1)}, u32[]{:S(2)}, u32[]{:S(2)}) collective-permute-start(bf16[7168,512]{1,0:T(8,128)(2,1)} %bitcast.52), channel_id=1, source_target_pairs={{0,64},{64,0},{1,65},{65,1},{2,66},{66,2},{3,67},{67,3},{4,68},{68... | collective-permute-start | bytes 22020104 | tf_op jit(solution)/shard_map/ppermute | solution.py:21
  1.2 62.8 %collective-permute-start = (bf16[7168,512]{1,0:T(8,128)(2,1)}, bf16[7168,512]{1,0:T(8,128)(2,1)S(1)}, u32[]{:S(2)}, u32[]{:S(2)}) collective-permute-start(bf16[7168,512]{1,0:T(8,128)(2,1)} %bitcast.49), channel_id=1, source_target_pairs={{0,64},{64,0},{1,65},{65,1},{2,66},{66,2},{3,67},{67,3},{4,68},{68... | collective-permute-start | bytes 22020104 | tf_op jit(solution)/shard_map/ppermute | solution.py:21
  1.3 0.9 copy-start.3
  2.3 0.7 copy-start.4
  2.9 0.7 copy-start.5
  65.2 7.4 %slice-start = ((s8[7340032]{0:T(1024)(128)(4,1)}), s8[4194304]{0:T(1024)(128)(4,1)S(1)}, s32[]{:S(2)}) async-start(s8[7340032]{0:T(1024)(128)(4,1)} %bitcast.50), calls=%async_computation.2 | async-start | bytes 8388608
  67.3 2.2 %copy-start = (bf16[1,2,1024,576]{2,3,1,0:T(8,128)(2,1)S(1)}, bf16[1,2,1024,576]{2,3,1,0:T(8,128)(2,1)}, u32[]{:S(2)}) copy-start(bf16[1,2,1024,576]{2,3,1,0:T(8,128)(2,1)} %param.16) | copy-start | bytes 7077892
  67.4 2.2 %copy-start.1 = (bf16[1,2,128,576]{2,3,1,0:T(8,128)(2,1)S(1)}, bf16[1,2,128,576]{2,3,1,0:T(8,128)(2,1)}, u32[]{:S(2)}) copy-start(bf16[1,2,128,576]{2,3,1,0:T(8,128)(2,1)} %param.15) | copy-start | bytes 884740
  67.4 2.2 %copy-start.2 = (s32[1,2]{1,0:T(1,128)S(1)}, s32[1,2]{1,0:T(1,128)}, u32[]{:S(2)}) copy-start(s32[1,2]{1,0:T(1,128)} %param.17) | copy-start | bytes 28
  67.4 5.2 %slice-start.1 = ((s8[7340032]{0:T(1024)(128)(4,1)}), s8[3145728]{0:T(1024)(128)(4,1)S(1)}, s32[]{:S(2)}) async-start(s8[7340032]{0:T(1024)(128)(4,1)} %bitcast.50), calls=%async_computation.3 | async-start | bytes 6291456
  69.6 5.2 %slice-start.2 = ((s8[7340032]{0:T(1024)(128)(4,1)}), s8[4194304]{0:T(1024)(128)(4,1)S(1)}, s32[]{:S(2)}) async-start(s8[7340032]{0:T(1024)(128)(4,1)} %bitcast.53), calls=%async_computation.4 | async-start | bytes 8388608
  72.6 2.2 %slice-start.3 = ((s8[7340032]{0:T(1024)(128)(4,1)}), s8[3145728]{0:T(1024)(128)(4,1)S(1)}, s32[]{:S(2)}) async-start(s8[7340032]{0:T(1024)(128)(4,1)} %bitcast.53), calls=%async_computation.5 | async-start | bytes 6291456
  72.6 4.4 %slice-start.4 = ((s8[7340032]{0:T(1024)(128)(4,1)}), s8[4194304]{0:T(1024)(128)(4,1)S(1)}, s32[]{:S(2)}) async-start(s8[7340032]{0:T(1024)(128)(4,1)} %bitcast.56), calls=%async_computation.6 | async-start | bytes 8388608
  74.8 2.2 %slice-start.5 = ((s8[7340032]{0:T(1024)(128)(4,1)}), s8[3145728]{0:T(1024)(128)(4,1)S(1)}, s32[]{:S(2)}) async-start(s8[7340032]{0:T(1024)(128)(4,1)} %bitcast.56), calls=%async_computation.7 | async-start | bytes 6291456

commit v5 on v4

--- a/solution.py
+++ b/solution.py
@@ -26,15 +26,22 @@
 
 
 def attention_body(lengths_ref, queries_ref, cache_ref, out_ref):
-    for r in range(queries_ref.shape[0]):
-        heads = queries_ref[r].astype(F32).T.astype(BF16)
-        scores = dot32(heads, cache_ref[r]) * qk_scale
-        valid = iota(scores.shape, 1) < lengths_ref[r]
-        scores = jnp.where(valid, scores, -jnp.inf)
-        peak = jnp.max(scores, axis=1, keepdims=True)
-        expo = jnp.where(valid, jnp.exp(scores - peak), 0.0)
-        probs = expo / jnp.sum(expo, axis=1, keepdims=True)
-        out_ref[r] = dot32(cache_ref[r, :LAT, :], probs.T.astype(BF16)).T.astype(BF16)
+    requests = range(queries_ref.shape[0])
+    heads = [queries_ref[r].astype(F32).T.astype(BF16) for r in requests]
+    scores = [dot32(heads[r], cache_ref[r]) for r in requests]
+    expos = []
+    for r in requests:
+        valid = iota(scores[r].shape, 1) < lengths_ref[r]
+        used = jnp.where(valid, scores[r], -jnp.inf)
+        expos.append(jnp.exp((used - jnp.max(used, axis=1, keepdims=True)) * qk_scale))
+    for r in requests:
+        summed = lax.dot_general(
+            expos[r].astype(BF16),
+            cache_ref[r, :LAT, :],
+            (((1,), (1,)), ((), ())),
+            preferred_element_type=F32,
+        )
+        out_ref[r] = (summed / jnp.sum(expos[r], axis=1, keepdims=True)).astype(BF16)
 
 
 def attention(queries, cache, lengths):

time: 136 us -> 136 us (level)
  no operation moved by 1% of the time
where the time goes in v5:
time: 136 us
  blocking collectives  111 us (82%)
  matrix products  13.1 us (10%)
  Pallas kernels  7.89 us (6%)
  local copies, waits for them, and re-layouts  2.37 us (2%)
    all_to_all x1, blocking collectives, per_device(): raw = lax.all_to_all(outgoing, 'dev', 0, 0, tiled=True)  58.8 us
    all_to_all x1, blocking collectives, per_device(): back = lax.all_to_all(leaving, 'dev', 0, 0, tiled=True)  51.9 us
    dot_general x8, matrix products, dot32(): return jnp.dot(left, right, preferred_element_type=F32)  13.1 us
    pallas_call x5, Pallas kernels, local_call(): pl.pallas_call(body, out_shape=out, in_specs=specs, out_specs=[pl.BlockSp...  7.89 us
  transfers between devices with their start and end apart: 3, of which 0 were waited for; matrix products, arithmetic and copies ran while one was open for 0% of the time, Pallas kernels for 1%

profile of v5, /device:TPU:0, one launch (start us, length us, event | category | flops | bytes accessed | tf_op | source)
XLA Modules:
  0.0 135.6 jit_solution(8582789840610207325)
XLA Ops:
  0.6 0.1 collective-permute-start.2
  0.7 0.5 collective-permute-start.1
  1.2 0.1 collective-permute-start
  1.3 0.0 copy-start.3
  1.3 0.9 copy-done.3
  2.3 0.0 copy-start.4
  2.3 0.7 copy-done.4
  2.9 0.0 copy-start.5
  2.9 0.7 copy-done.5
  3.6 1.6 %shard_map.104 = (bf16[1024,1792]{1,0:T(8,128)(2,1)S(1)}, bf16[128,1024]{1,0:T(8,128)(2,1)S(1)}) custom-call(s32[8,16]{1,0:T(8,128)S(1)} %bitcast.45, f32[8,16]{1,0:T(8,128)S(1)} %bitcast.46, bf16[16,7168]{1,0:T(8,128)(2,1)S(1)} %bitcast.44), custom_call_target="tpu_custom_call" | custom-call | flops 234881024 | bytes 4162560 | tf_op jit(solution)/shard_map/pallas_call | solution.py:67
  5.2 58.8 %all_to_all.23 = bf16[64,16,1792]{2,1,0:T(8,128)(2,1)S(1)} all-to-all(bf16[64,16,1792]{2,1,0:T(8,128)(2,1)S(1)} %bitcast.40), channel_id=1, replica_groups=mesh['section'=2,'dev'=64] {'dev'}, dimensions={0} | all-to-all | bytes 7340032 | tf_op jit(solution)/shard_map/all_to_all | solution.py:209
  64.0 0.0 collective-permute-done.2
  64.0 0.0 collective-permute-done.1
  64.0 0.0 collective-permute-done
  64.0 1.1 shard_map.105
  65.2 0.0 slice-start
  65.2 2.1 %fusion.8 = f32[256,512]{1,0:T(8,128)S(1)} fusion(bf16[256,7168]{1,0:T(8,128)(2,1)S(1)} %shard_map.105, bf16[7168,512]{1,0:T(8,128)(2,1)S(1)} %collective-permute-done), kind=kOutput, calls=%fused_computation.14 | convolution fusion | flops 1879048192 | bytes 11534336 | tf_op jit(solution)/shard_map/dot_general | solution.py:25
  67.3 0.0 copy-start
  67.4 0.0 copy-start.1
  67.4 0.0 copy-start.2
  67.4 0.0 slice-start.1
  67.4 2.2 %multiply_convert_fusion = bf16[256,512]{1,0:T(8,128)(2,1)S(1)} fusion(f32[256,512]{1,0:T(8,128)S(1)} %fusion.8, bf16[256,7168]{1,0:T(8,128)(2,1)S(1)} %shard_map.105, bf16[7168,512]{1,0:T(8,128)(2,1)S(1)} %collective-permute-done.1), kind=kOutput, calls=%fused_computation.10 | convolution fusion | flops 1879834624 | bytes 11796480 | tf_op jit(solution)/shard_map/dot_general | solution.py:25
  69.6 0.0 copy-done
  69.6 0.0 copy-done.1
  69.6 0.0 copy-done.2
  69.6 0.0 slice-start.2
  69.6 2.6 %shard_map.106 = bf16[2,128,512]{2,1,0:T(8,128)(2,1)} custom-call(s32[2]{0:T(128)S(1)} %bitcast.43, bf16[2,576,128]{2,1,0:T(8,128)(2,1)S(1)} %bitcast.42, bf16[2,576,1024]{2,1,0:T(8,128)(2,1)S(1)} %bitcast.41), custom_call_target="tpu_custom_call" | custom-call | flops 603979776 | bytes 2916360 | tf_op jit(solution)/shard_map/pallas_call | solution.py:67
  72.2 0.0 slice-done
  72.3 0.0 slice-done.1
  72.3 0.0 slice-start.3
  72.3 0.0 slice-start.4
  72.3 2.1 %fusion.6 = f32[256,512]{1,0:T(8,128)S(1)} fusion(bf16[256,7168]{1,0:T(8,128)(2,1)S(1)} %shard_map.105, bf16[1,7168,512]{2,1,0:T(8,128)(2,1)S(1)} %bitcast.51), kind=kOutput, calls=%fused_computation.12 | convolution fusion | flops 1879048192 | bytes 11534336 | tf_op jit(solution)/shard_map/dot_general | solution.py:25
  74.4 0.0 slice-done.2
  74.4 0.0 slice-done.3
  74.5 0.0 slice-start.5
  74.5 2.2 %fusion.4 = bf16[256,512]{1,0:T(8,128)(2,1)S(1)} fusion(bf16[256,7168]{1,0:T(8,128)(2,1)S(1)} %shard_map.105, f32[256,512]{1,0:T(8,128)S(1)} %fusion.6, bf16[1,7168,512]{2,1,0:T(8,128)(2,1)S(1)} %bitcast.54), kind=kOutput, calls=%fused_computation.9 | convolution fusion | flops 1879834624 | bytes 11796480 | tf_op jit(solution)/shard_map/dot_general | solution.py:25
  76.6 0.0 slice-done.4
  76.6 0.0 slice-done.5
  76.7 1.1 convolution_convert_fusion.refs_3_
  77.8 1.1 convolution_convert_fusion.1.refs_2_
  78.9 1.1 convolution_convert_fusion.2.refs_1_
  80.1 1.1 convolution_convert_fusion.3.refs_0_
  81.2 1.2 shard_map.107
  82.4 51.9 %all_to_all.24 = bf16[64,16,1792]{2,1,0:T(8,128)(2,1)S(1)} all-to-all(bf16[64,16,1792]{2,1,0:T(8,128)(2,1)S(1)} %bitcast.39), channel_id=1, replica_groups=mesh['section'=2,'dev'=64] {'dev'}, dimensions={0} | all-to-all | bytes 7340032 | tf_op jit(solution)/shard_map/all_to_all | solution.py:237
  134.3 1.3 shard_map.108
  (3 shorter events, 0.0 us)
Async XLA Ops:
  0.6 63.4 %collective-permute-start.2 = (bf16[512,7168]{1,0:T(8,128)(2,1)}, bf16[512,7168]{1,0:T(8,128)(2,1)S(1)}, u32[]{:S(2)}, u32[]{:S(2)}) collective-permute-start(bf16[512,7168]{1,0:T(8,128)(2,1)} %bitcast.55), channel_id=1, source_target_pairs={{0,64},{64,0},{1,65},{65,1},{2,66},{66,2},{3,67},{67,3},{4,68},{68... | collective-permute-start | bytes 22020104 | tf_op jit(solution)/shard_map/ppermute | solution.py:21
  0.7 63.3 %collective-permute-start.1 = (bf16[7168,512]{1,0:T(8,128)(2,1)}, bf16[7168,512]{1,0:T(8,128)(2,1)S(1)}, u32[]{:S(2)}, u32[]{:S(2)}) collective-permute-start(bf16[7168,512]{1,0:T(8,128)(2,1)} %bitcast.52), channel_id=1, source_target_pairs={{0,64},{64,0},{1,65},{65,1},{2,66},{66,2},{3,67},{67,3},{4,68},{68... | collective-permute-start | bytes 22020104 | tf_op jit(solution)/shard_map/ppermute | solution.py:21
  1.2 62.8 %collective-permute-start = (bf16[7168,512]{1,0:T(8,128)(2,1)}, bf16[7168,512]{1,0:T(8,128)(2,1)S(1)}, u32[]{:S(2)}, u32[]{:S(2)}) collective-permute-start(bf16[7168,512]{1,0:T(8,128)(2,1)} %bitcast.49), channel_id=1, source_target_pairs={{0,64},{64,0},{1,65},{65,1},{2,66},{66,2},{3,67},{67,3},{4,68},{68... | collective-permute-start | bytes 22020104 | tf_op jit(solution)/shard_map/ppermute | solution.py:21
  1.3 0.9 copy-start.3
  2.3 0.7 copy-start.4
  2.9 0.7 copy-start.5
  65.2 7.1 %slice-start = ((s8[7340032]{0:T(1024)(128)(4,1)}), s8[4194304]{0:T(1024)(128)(4,1)S(1)}, s32[]{:S(2)}) async-start(s8[7340032]{0:T(1024)(128)(4,1)} %bitcast.50), calls=%async_computation.2 | async-start | bytes 8388608
  67.3 2.2 %copy-start = (bf16[1,2,1024,576]{2,3,1,0:T(8,128)(2,1)S(1)}, bf16[1,2,1024,576]{2,3,1,0:T(8,128)(2,1)}, u32[]{:S(2)}) copy-start(bf16[1,2,1024,576]{2,3,1,0:T(8,128)(2,1)} %param.16) | copy-start | bytes 7077892
  67.4 2.2 %copy-start.1 = (bf16[1,2,128,576]{2,3,1,0:T(8,128)(2,1)S(1)}, bf16[1,2,128,576]{2,3,1,0:T(8,128)(2,1)}, u32[]{:S(2)}) copy-start(bf16[1,2,128,576]{2,3,1,0:T(8,128)(2,1)} %param.15) | copy-start | bytes 884740
  67.4 2.2 %copy-start.2 = (s32[1,2]{1,0:T(1,128)S(1)}, s32[1,2]{1,0:T(1,128)}, u32[]{:S(2)}) copy-start(s32[1,2]{1,0:T(1,128)} %param.17) | copy-start | bytes 28
  67.4 4.9 %slice-start.1 = ((s8[7340032]{0:T(1024)(128)(4,1)}), s8[3145728]{0:T(1024)(128)(4,1)S(1)}, s32[]{:S(2)}) async-start(s8[7340032]{0:T(1024)(128)(4,1)} %bitcast.50), calls=%async_computation.3 | async-start | bytes 6291456
  69.6 4.8 %slice-start.2 = ((s8[7340032]{0:T(1024)(128)(4,1)}), s8[4194304]{0:T(1024)(128)(4,1)S(1)}, s32[]{:S(2)}) async-start(s8[7340032]{0:T(1024)(128)(4,1)} %bitcast.53), calls=%async_computation.4 | async-start | bytes 8388608
  72.3 2.2 %slice-start.3 = ((s8[7340032]{0:T(1024)(128)(4,1)}), s8[3145728]{0:T(1024)(128)(4,1)S(1)}, s32[]{:S(2)}) async-start(s8[7340032]{0:T(1024)(128)(4,1)} %bitcast.53), calls=%async_computation.5 | async-start | bytes 6291456
  72.3 4.4 %slice-start.4 = ((s8[7340032]{0:T(1024)(128)(4,1)}), s8[4194304]{0:T(1024)(128)(4,1)S(1)}, s32[]{:S(2)}) async-start(s8[7340032]{0:T(1024)(128)(4,1)} %bitcast.56), calls=%async_computation.6 | async-start | bytes 8388608
  74.5 2.2 %slice-start.5 = ((s8[7340032]{0:T(1024)(128)(4,1)}), s8[3145728]{0:T(1024)(128)(4,1)S(1)}, s32[]{:S(2)}) async-start(s8[7340032]{0:T(1024)(128)(4,1)} %bitcast.56), calls=%async_computation.7 | async-start | bytes 6291456

commit v6 on v5

--- a/solution.py
+++ b/solution.py
@@ -27,8 +27,12 @@
 
 def attention_body(lengths_ref, queries_ref, cache_ref, out_ref):
     requests = range(queries_ref.shape[0])
-    heads = [queries_ref[r].astype(F32).T.astype(BF16) for r in requests]
-    scores = [dot32(heads[r], cache_ref[r]) for r in requests]
+    scores = [
+        lax.dot_general(
+            queries_ref[r], cache_ref[r], (((0,), (0,)), ((), ())), preferred_element_type=F32
+        )
+        for r in requests
+    ]
     expos = []
     for r in requests:
         valid = iota(scores[r].shape, 1) < lengths_ref[r]

time: 136 us -> 136 us (level)
  no operation moved by 1% of the time
where the time goes in v6:
time: 136 us
  blocking collectives  111 us (82%)
  matrix products  13.1 us (10%)
  Pallas kernels  7.88 us (6%)
  local copies, waits for them, and re-layouts  2.37 us (2%)
    all_to_all x1, blocking collectives, per_device(): raw = lax.all_to_all(outgoing, 'dev', 0, 0, tiled=True)  58.8 us
    all_to_all x1, blocking collectives, per_device(): back = lax.all_to_all(leaving, 'dev', 0, 0, tiled=True)  51.9 us
    dot_general x8, matrix products, dot32(): return jnp.dot(left, right, preferred_element_type=F32)  13.1 us
    pallas_call x5, Pallas kernels, local_call(): pl.pallas_call(body, out_shape=out, in_specs=specs, out_specs=[pl.BlockSp...  7.88 us
  transfers between devices with their start and end apart: 3, of which 0 were waited for; matrix products, arithmetic and copies ran while one was open for 0% of the time, Pallas kernels for 1%

profile of v6, /device:TPU:0, one launch (start us, length us, event | category | flops | bytes accessed | tf_op | source)
XLA Modules:
  0.0 135.6 jit_solution(15358961951498990907)
XLA Ops:
  0.6 0.1 collective-permute-start.2
  0.7 0.5 collective-permute-start.1
  1.2 0.1 collective-permute-start
  1.3 0.0 copy-start.3
  1.3 0.9 copy-done.3
  2.3 0.0 copy-start.4
  2.3 0.7 copy-done.4
  2.9 0.0 copy-start.5
  2.9 0.7 copy-done.5
  3.6 1.6 %shard_map.104 = (bf16[1024,1792]{1,0:T(8,128)(2,1)S(1)}, bf16[128,1024]{1,0:T(8,128)(2,1)S(1)}) custom-call(s32[8,16]{1,0:T(8,128)S(1)} %bitcast.45, f32[8,16]{1,0:T(8,128)S(1)} %bitcast.46, bf16[16,7168]{1,0:T(8,128)(2,1)S(1)} %bitcast.44), custom_call_target="tpu_custom_call" | custom-call | flops 234881024 | bytes 4162560 | tf_op jit(solution)/shard_map/pallas_call | solution.py:71
  5.2 58.8 %all_to_all.23 = bf16[64,16,1792]{2,1,0:T(8,128)(2,1)S(1)} all-to-all(bf16[64,16,1792]{2,1,0:T(8,128)(2,1)S(1)} %bitcast.40), channel_id=1, replica_groups=mesh['section'=2,'dev'=64] {'dev'}, dimensions={0} | all-to-all | bytes 7340032 | tf_op jit(solution)/shard_map/all_to_all | solution.py:213
  64.0 0.0 collective-permute-done.2
  64.0 0.0 collective-permute-done.1
  64.0 0.0 collective-permute-done
  64.0 1.1 shard_map.105
  65.2 0.0 slice-start
  65.2 2.1 %fusion.8 = f32[256,512]{1,0:T(8,128)S(1)} fusion(bf16[256,7168]{1,0:T(8,128)(2,1)S(1)} %shard_map.105, bf16[7168,512]{1,0:T(8,128)(2,1)S(1)} %collective-permute-done), kind=kOutput, calls=%fused_computation.14 | convolution fusion | flops 1879048192 | bytes 11534336 | tf_op jit(solution)/shard_map/dot_general | solution.py:25
  67.3 0.0 copy-start
  67.4 0.0 copy-start.1
  67.4 0.0 copy-start.2
  67.4 0.0 slice-start.1
  67.4 2.2 %multiply_convert_fusion = bf16[256,512]{1,0:T(8,128)(2,1)S(1)} fusion(f32[256,512]{1,0:T(8,128)S(1)} %fusion.8, bf16[256,7168]{1,0:T(8,128)(2,1)S(1)} %shard_map.105, bf16[7168,512]{1,0:T(8,128)(2,1)S(1)} %collective-permute-done.1), kind=kOutput, calls=%fused_computation.10 | convolution fusion | flops 1879834624 | bytes 11796480 | tf_op jit(solution)/shard_map/dot_general | solution.py:25
  69.6 0.0 copy-done
  69.6 0.0 copy-done.1
  69.6 0.0 copy-done.2
  69.6 0.0 slice-start.2
  69.6 2.6 %shard_map.106 = bf16[2,128,512]{2,1,0:T(8,128)(2,1)} custom-call(s32[2]{0:T(128)S(1)} %bitcast.43, bf16[2,576,128]{2,1,0:T(8,128)(2,1)S(1)} %bitcast.42, bf16[2,576,1024]{2,1,0:T(8,128)(2,1)S(1)} %bitcast.41), custom_call_target="tpu_custom_call" | custom-call | flops 603979776 | bytes 2916360 | tf_op jit(solution)/shard_map/pallas_call | solution.py:71
  72.2 0.0 slice-done
  72.2 0.0 slice-done.1
  72.2 0.0 slice-start.3
  72.2 0.0 slice-start.4
  72.3 2.1 %fusion.6 = f32[256,512]{1,0:T(8,128)S(1)} fusion(bf16[256,7168]{1,0:T(8,128)(2,1)S(1)} %shard_map.105, bf16[1,7168,512]{2,1,0:T(8,128)(2,1)S(1)} %bitcast.51), kind=kOutput, calls=%fused_computation.12 | convolution fusion | flops 1879048192 | bytes 11534336 | tf_op jit(solution)/shard_map/dot_general | solution.py:25
  74.4 0.0 slice-done.2
  74.4 0.0 slice-done.3
  74.4 0.0 slice-start.5
  74.5 2.2 %fusion.4 = bf16[256,512]{1,0:T(8,128)(2,1)S(1)} fusion(bf16[256,7168]{1,0:T(8,128)(2,1)S(1)} %shard_map.105, f32[256,512]{1,0:T(8,128)S(1)} %fusion.6, bf16[1,7168,512]{2,1,0:T(8,128)(2,1)S(1)} %bitcast.54), kind=kOutput, calls=%fused_computation.9 | convolution fusion | flops 1879834624 | bytes 11796480 | tf_op jit(solution)/shard_map/dot_general | solution.py:25
  76.6 0.0 slice-done.4
  76.6 0.0 slice-done.5
  76.7 1.1 convolution_convert_fusion.refs_3_
  77.8 1.1 convolution_convert_fusion.1.refs_2_
  78.9 1.1 convolution_convert_fusion.2.refs_1_
  80.0 1.1 convolution_convert_fusion.3.refs_0_
  81.2 1.2 shard_map.107
  82.4 51.9 %all_to_all.24 = bf16[64,16,1792]{2,1,0:T(8,128)(2,1)S(1)} all-to-all(bf16[64,16,1792]{2,1,0:T(8,128)(2,1)S(1)} %bitcast.39), channel_id=1, replica_groups=mesh['section'=2,'dev'=64] {'dev'}, dimensions={0} | all-to-all | bytes 7340032 | tf_op jit(solution)/shard_map/all_to_all | solution.py:241
  134.3 1.3 shard_map.108
  (3 shorter events, 0.0 us)
Async XLA Ops:
  0.6 63.4 %collective-permute-start.2 = (bf16[512,7168]{1,0:T(8,128)(2,1)}, bf16[512,7168]{1,0:T(8,128)(2,1)S(1)}, u32[]{:S(2)}, u32[]{:S(2)}) collective-permute-start(bf16[512,7168]{1,0:T(8,128)(2,1)} %bitcast.55), channel_id=1, source_target_pairs={{0,64},{64,0},{1,65},{65,1},{2,66},{66,2},{3,67},{67,3},{4,68},{68... | collective-permute-start | bytes 22020104 | tf_op jit(solution)/shard_map/ppermute | solution.py:21
  0.7 63.3 %collective-permute-start.1 = (bf16[7168,512]{1,0:T(8,128)(2,1)}, bf16[7168,512]{1,0:T(8,128)(2,1)S(1)}, u32[]{:S(2)}, u32[]{:S(2)}) collective-permute-start(bf16[7168,512]{1,0:T(8,128)(2,1)} %bitcast.52), channel_id=1, source_target_pairs={{0,64},{64,0},{1,65},{65,1},{2,66},{66,2},{3,67},{67,3},{4,68},{68... | collective-permute-start | bytes 22020104 | tf_op jit(solution)/shard_map/ppermute | solution.py:21
  1.2 62.8 %collective-permute-start = (bf16[7168,512]{1,0:T(8,128)(2,1)}, bf16[7168,512]{1,0:T(8,128)(2,1)S(1)}, u32[]{:S(2)}, u32[]{:S(2)}) collective-permute-start(bf16[7168,512]{1,0:T(8,128)(2,1)} %bitcast.49), channel_id=1, source_target_pairs={{0,64},{64,0},{1,65},{65,1},{2,66},{66,2},{3,67},{67,3},{4,68},{68... | collective-permute-start | bytes 22020104 | tf_op jit(solution)/shard_map/ppermute | solution.py:21
  1.3 0.9 copy-start.3
  2.3 0.7 copy-start.4
  2.9 0.7 copy-start.5
  65.2 7.1 %slice-start = ((s8[7340032]{0:T(1024)(128)(4,1)}), s8[4194304]{0:T(1024)(128)(4,1)S(1)}, s32[]{:S(2)}) async-start(s8[7340032]{0:T(1024)(128)(4,1)} %bitcast.50), calls=%async_computation.2 | async-start | bytes 8388608
  67.3 2.2 %copy-start = (bf16[1,2,1024,576]{2,3,1,0:T(8,128)(2,1)S(1)}, bf16[1,2,1024,576]{2,3,1,0:T(8,128)(2,1)}, u32[]{:S(2)}) copy-start(bf16[1,2,1024,576]{2,3,1,0:T(8,128)(2,1)} %param.16) | copy-start | bytes 7077892
  67.4 2.2 %copy-start.1 = (bf16[1,2,128,576]{2,3,1,0:T(8,128)(2,1)S(1)}, bf16[1,2,128,576]{2,3,1,0:T(8,128)(2,1)}, u32[]{:S(2)}) copy-start(bf16[1,2,128,576]{2,3,1,0:T(8,128)(2,1)} %param.15) | copy-start | bytes 884740
  67.4 2.2 %copy-start.2 = (s32[1,2]{1,0:T(1,128)S(1)}, s32[1,2]{1,0:T(1,128)}, u32[]{:S(2)}) copy-start(s32[1,2]{1,0:T(1,128)} %param.17) | copy-start | bytes 28
  67.4 4.9 %slice-start.1 = ((s8[7340032]{0:T(1024)(128)(4,1)}), s8[3145728]{0:T(1024)(128)(4,1)S(1)}, s32[]{:S(2)}) async-start(s8[7340032]{0:T(1024)(128)(4,1)} %bitcast.50), calls=%async_computation.3 | async-start | bytes 6291456
  69.6 4.8 %slice-start.2 = ((s8[7340032]{0:T(1024)(128)(4,1)}), s8[4194304]{0:T(1024)(128)(4,1)S(1)}, s32[]{:S(2)}) async-start(s8[7340032]{0:T(1024)(128)(4,1)} %bitcast.53), calls=%async_computation.4 | async-start | bytes 8388608
  72.2 2.2 %slice-start.3 = ((s8[7340032]{0:T(1024)(128)(4,1)}), s8[3145728]{0:T(1024)(128)(4,1)S(1)}, s32[]{:S(2)}) async-start(s8[7340032]{0:T(1024)(128)(4,1)} %bitcast.53), calls=%async_computation.5 | async-start | bytes 6291456
  72.2 4.4 %slice-start.4 = ((s8[7340032]{0:T(1024)(128)(4,1)}), s8[4194304]{0:T(1024)(128)(4,1)S(1)}, s32[]{:S(2)}) async-start(s8[7340032]{0:T(1024)(128)(4,1)} %bitcast.56), calls=%async_computation.6 | async-start | bytes 8388608
  74.4 2.2 %slice-start.5 = ((s8[7340032]{0:T(1024)(128)(4,1)}), s8[3145728]{0:T(1024)(128)(4,1)S(1)}, s32[]{:S(2)}) async-start(s8[7340032]{0:T(1024)(128)(4,1)} %bitcast.56), calls=%async_computation.7 | async-start | bytes 6291456
